TPU v7x, 256 devices: a whole 4x4x8 slice. The times are simulated.
256 devices in a mesh: leaf: 64 (over y, z, core), vec: 4 (over x).
Axes of the slice: x: 4, y: 4, z: 8, core: 2. Of those that a mesh axis runs over, the one named last changes fastest.
Arguments:
- points_x: float32 [16, 262144], P('vec', 'leaf'), may hold values from -6 to 6
- near_list: int32 [4096, 8], P('leaf'), may hold values from 0 to 4095, as said below
- near_blocks: float32 [8, 64, 262144], P('vec', None, 'leaf'), may hold values from -0.25 to 0.25
- leaf_basis: float32 [32, 262144], P(None, 'leaf'), may hold values from -0.75 to 0.75
- out_basis: float32 [32, 262144], P(None, 'leaf'), may hold values from -1 to 1
- up_transfer: float32 [32, 131072], P(None, 'leaf'), may hold values from -0.375 to 0.375
- down_transfer: float32 [32, 131072], P(None, 'leaf'), may hold values from -1 to 1
- send_leaves: int32 [64, 64, 8], P('leaf'), may hold values from 0 to 63, as said below
- send_counts: int32 [64, 64], P('leaf'), may hold values from 1 to 8, as said below
- recv_slot: int32 [4096, 16], P('leaf'), may hold values from 0 to 511
- leaf_coupling: float32 [16, 32, 131072], P(None, None, 'leaf'), may hold values from -0.25 to 0.25
- top_list: int32 [512, 8], P('leaf'), may hold values from 0 to 511
- top_coupling: float32 [8, 32, 16384], P(None, None, 'leaf'), may hold values from -0.375 to 0.375
Outputs:
- product: float32 [16, 262144], P('vec', 'leaf')
Inputs may be any that keep to these rules, and one draw needn't show every extreme that they name: `near_list`: the 8 source leaves of a target leaf lie on the target's own device or on the devices just before and after it along leaf. The 8 entries of send_leaves[p, d] are distinct local leaves of device p. `send_counts`: every sender fills all 8 slots toward some receiver, and some receiver gets all 8 slots filled from every sender.
All inputs are finite; a program needn't handle non-finite values.
Results may differ from a plain program's by a relative error of at most 0.000058.
Values sent between devices are 32-bit elements; how exact they have to be, the bound alone decides.
No kernel may reach another device: no remote copies, remote signals or barrier semaphores. Data moves between devices by JAX's collectives and lax.ppermute only.
A program may use at most 128 MiB of HBM per device.

v0:
```python
import jax
import jax.numpy as jnp
from jax import lax
from jax.sharding import PartitionSpec as P

PTS = 64
RANK = 32


def padded_2(array, sides, width):
    for axis, dim in sides:
        size, length = (lax.axis_size(axis), array.shape[dim])
        up = [(i, (i + 1) % size) for i in range(size - 1)]
        down = [(j, i) for i, j in up]
        last = lax.slice_in_dim(array, length - width, length, axis=dim)
        leading = lax.slice_in_dim(array, 0, width, axis=dim)
        before = lax.ppermute(last, axis, up)
        after = lax.ppermute(leading, axis, down)
        array = jnp.concatenate([before, array, after], axis=dim)
    return array


def contract(pattern, left, right):
    return jnp.einsum(pattern, left, right, precision=lax.Precision.HIGHEST)


def local(
    points_x,
    near_list,
    near_blocks,
    leaf_basis,
    out_basis,
    up_transfer,
    down_transfer,
    send_leaves,
    send_counts,
    recv_slot,
    leaf_coupling,
    top_list,
    top_coupling,
):
    columns = points_x.shape[0]
    leaf_count = near_list.shape[0]
    par_count = top_list.shape[0]
    far_count = recv_slot.shape[1]
    top_count = top_list.shape[1]
    slot_count = send_leaves.shape[2]
    peer_total = lax.axis_size("leaf")
    leaf_index = lax.axis_index("leaf")
    vectors = points_x.reshape(columns, leaf_count, PTS)
    skeleton = contract("clp,rlp->lcr", vectors, leaf_basis.reshape(RANK, leaf_count, PTS))
    tile_flat = skeleton.reshape(leaf_count, columns * RANK)
    lifted = contract("lcr,rlq->lcq", skeleton, up_transfer.reshape(RANK, leaf_count, RANK))
    parents = (
        lifted.reshape(par_count, 8, columns, RANK).sum(axis=1).reshape(par_count, columns * RANK)
    )
    all_parents = lax.all_gather(parents, "leaf", axis=0, tiled=True)
    live_slot = jnp.arange(slot_count, dtype=jnp.int32)[None, :] < send_counts[0][:, None]
    sender_ids = jnp.where(live_slot, send_leaves[0] + leaf_index * leaf_count, -1)
    received_ids = lax.all_to_all(
        sender_ids, "leaf", split_axis=0, concat_axis=0, tiled=True
    ).reshape(peer_total * slot_count)
    every_tile = lax.all_gather(tile_flat, "leaf", axis=0, tiled=True)
    wanted = received_ids[recv_slot]
    gathered = jnp.where(wanted[:, :, None] >= 0, every_tile[jnp.maximum(wanted, 0)], 0.0)
    gathered = gathered.reshape(leaf_count, far_count, columns, RANK)
    coupled = contract(
        "ljcr,jrlq->lcq", gathered, leaf_coupling.reshape(far_count, RANK, leaf_count, RANK)
    )
    top_tiles = all_parents[top_list].reshape(par_count, top_count, columns, RANK)
    top_field = contract(
        "qjcr,jrqs->qcs", top_tiles, top_coupling.reshape(top_count, RANK, par_count, RANK)
    )
    spread = jnp.repeat(top_field, 8, axis=0)
    down_part = contract("lcr,rlq->lcq", spread, down_transfer.reshape(RANK, leaf_count, RANK))
    local_field = coupled + down_part
    far_out = contract("lcr,rlp->clp", local_field, out_basis.reshape(RANK, leaf_count, PTS))
    share_count = near_blocks.shape[0]
    source = lax.all_gather(points_x, "vec", axis=0, tiled=True)
    padded = padded_2(source, (("leaf", 1),), leaf_count * PTS)
    padded = padded.reshape(source.shape[0], 3 * leaf_count, PTS)
    relative = near_list - (leaf_index - 1) * leaf_count
    my_rows = lax.dynamic_slice_in_dim(
        relative, lax.axis_index("vec") * share_count, share_count, 1
    )
    picked = padded[:, my_rows]
    partial_value = contract(
        "cljs,jslp->clp", picked, near_blocks.reshape(share_count, PTS, leaf_count, PTS)
    )
    near_out = lax.psum_scatter(
        partial_value.reshape(source.shape[0], leaf_count * PTS),
        "vec",
        scatter_dimension=0,
        tiled=True,
    )
    return far_out.reshape(columns, leaf_count * PTS) + near_out


def solution(mesh):
    placed = (
        P("vec", "leaf"),
        P("leaf", None),
        P("vec", None, "leaf"),
        P(None, "leaf"),
        P(None, "leaf"),
        P(None, "leaf"),
        P(None, "leaf"),
        P("leaf", None, None),
        P("leaf", None),
        P("leaf", None),
        P(None, None, "leaf"),
        P("leaf", None),
        P(None, None, "leaf"),
    )
    return jax.shard_map(
        local, mesh=mesh, in_specs=placed, out_specs=P("vec", "leaf"), check_vma=False
    )
```

profile of v0, /device:TPU:8, one launch (start us, length us, event | category | flops | bytes accessed | tf_op | source)
XLA Modules:
  0.0 193.0 jit_solution(3936105275238533606)
XLA Ops:
  7.4 12.9 %all-gather = f32[4,4,4096]{2,1,0:T(4,128)S(1)} all-gather(f32[1,4,4096]{2,1,0:T(4,128)} %bitcast.31), channel_id=1, replica_groups=mesh['leaf'=64,'vec'=4] {'vec'}, dimensions={0}, use_global_device_ids=true | all-gather | bytes 327680 | tf_op jit(solution)/shard_map/all_gather | solution.py:79
  20.3 0.1 reshape.187
  20.4 1.9 collective-permute-start
  22.4 5.8 %collective-permute-start.1 = (f32[16,4096]{1,0:T(8,128)S(1)}, f32[16,4096]{1,0:T(8,128)}, u32[]{:S(2)}, u32[]{:S(2)}) collective-permute-start(f32[16,4096]{1,0:T(8,128)S(1)} %reshape.187), channel_id=1, source_target_pairs={{4,0},{8,4},{12,8},{16,12},{20,16},{24,20},{28,24},{32,28},{36,32}... | collective-permute-start | bytes 786440 | tf_op jit(solution)/shard_map/ppermute | solution.py:18
  28.1 1.0 reshape.123
  29.1 1.5 reshape.124
  30.5 2.3 %fusion.18 = f32[64,4,32]{2,1,0:T(4,128)S(1)} fusion(f32[32,64,64]{2,1,0:T(8,128)S(1)} %reshape.124, f32[4,64,64]{2,1,0:T(8,128)S(1)} %reshape.123), kind=kOutput, calls=%fused_computation.19 | convolution fusion | flops 6291456 | bytes 622592 | tf_op jit(solution)/shard_map/clp,rlp->lcr/dot_general | solution.py:24
  32.9 0.1 copy.39
  33.0 0.7 copy.40
  33.8 0.7 compare_select_fusion
  34.6 11.4 %all-to-all-start = ((s32[64,1,8]{2,1,0:T(1,128)}), s32[64,1,8]{2,1,0:T(1,128)}, u32[]{:S(2)}, u32[]{:S(2)}) async-start(s32[64,1,8]{2,1,0:T(1,128)} %compare_select_fusion), calls=%async_computation | async-start | bytes 65536 | tf_op jit(solution)/shard_map/all_to_all | solution.py:60
  46.1 0.1 copy.47
  46.2 0.6 reshape.165
  46.9 0.7 reshape.141
  47.6 0.3 reshape.127
  47.9 1.5 bitcast_reduce_fusion
  49.5 0.7 compare_select_fusion.2
  50.3 43.8 %all_gather.10 = f32[512,128]{1,0:T(8,128)S(1)} all-gather(f32[8,128]{1,0:T(8,128)S(1)} %reshape.129), channel_id=1, replica_groups=mesh['leaf'=64,'vec'=4] {'leaf'}, dimensions={0}, use_global_device_ids=true | all-gather | bytes 266240 | tf_op jit(solution)/shard_map/all_gather | solution.py:57
  94.1 0.6 gather_fusion.2
  94.7 0.1 reshape.130
  94.8 1.2 reshape.131
  96.0 0.8 convolution_bitcast_fusion.1
  96.8 0.7 broadcast_clamp_fusion
  97.5 0.6 pad_clamp_fusion
  98.1 3.0 %reshape.137 = f32[2,64,64,64]{3,2,1,0:T(8,128)} reshape(f32[2,64,4096]{2,1,0:T(8,128)S(1)} %copy-done.2) | data formatting | bytes 4194304 | tf_op jit(solution)/shard_map/reshape | solution.py:88
  101.1 11.4 %reshape.126 = f32[16,32,64,32]{3,2,1,0:T(8,128)} reshape(f32[16,32,2048]{2,1,0:T(8,128)} %param.23) | data formatting | bytes 8388608 | tf_op jit(solution)/shard_map/reshape | solution.py:68
  112.6 1.3 reshape.133
  113.9 1.4 reshape.134
  115.3 0.6 dynamic-slice
  116.5 0.5 broadcast.79
  117.0 1.4 reduce.3
  118.4 0.1 reshape.122
  118.5 6.9 %gather_fusion = s32[1024]{0:T(1024)S(1)} fusion(s32[512]{0:T(512)S(1)} %reshape.122, s32[1024]{0:T(1024)S(1)} %broadcast_clamp_fusion), kind=kCustom, calls=%fused_computation | custom fusion | bytes 12288 | tf_op jit(solution)/shard_map/gather | solution.py:64
  125.5 1.1 pad_maximum_fusion
  126.6 0.6 reshape.136
  127.2 0.9 copy.48
  128.1 0.8 gather_fusion.3
  128.9 8.3 %fusion.5 = f32[16,64,64]{2,0,1:T(8,128)S(1)} fusion(f32[16,64,2,64]{3,0,2,1:T(8,128)S(1)} %bitcast.29, f32[2,64,64,64]{3,2,1,0:T(8,128)} %reshape.137), kind=kOutput, calls=%fused_computation.9 | convolution fusion | flops 100663296 | bytes 2883584 | tf_op jit(solution)/shard_map/cljs,jslp->clp/dot_general | solution.py:24
  137.2 0.2 copy.50
  137.3 0.9 reshape.138
  138.3 4.4 %gather_fusion.1 = f32[1024,128]{1,0:T(8,128)S(1)} fusion(f32[4096,128]{1,0:T(8,128)} %all-gather.3.cloned.1.call-done, s32[1024]{0:T(1024)S(1)} %maximum_clamp_fusion), kind=kCustom, calls=%fused_computation.1 | custom fusion | bytes 1052672 | tf_op jit(solution)/shard_map/gather | solution.py:65
  142.7 0.9 gather.16
  143.6 19.2 %fusion.8 = f32[64,4,32]{2,1,0:T(4,128)S(1)} fusion(f32[16,32,64,32]{3,2,1,0:T(8,128)} %reshape.126, f32[64,16,4,32]{3,2,1,0:T(4,128)S(1)} %gather.16, pred[64,16]{1,0:T(8,128)(4,1)S(1)} %reshape.182), kind=kOutput, calls=%fused_computation.12 | convolution fusion | flops 50462720 | bytes 4752384 | tf_op jit(solution)/shard_map/ljcr,jrlq->lcq/dot_general | solution.py:24
  162.9 1.5 convolution_add_fusion
  164.4 1.5 convolution_bitcast_fusion
  165.9 0.1 reshape.135
  166.0 18.0 %all-reduce.3.cloned.1.call-done = f32[16,4096]{1,0:T(8,128)} async-done(((f32[16,4096]{1,0:T(8,128)}), f32[16,4096]{1,0:T(8,128)}) %all-reduce.3.cloned.1.call-update) | async-done | bytes 262160
  184.0 1.6 dynamic-slice_add_fusion
  (44 shorter events, 0.6 us)
Async XLA Ops:
  7.4 130.9 %all-gather.3.cloned.1.call-start = ((), (), s32[]{:S(2)}) async-start(), calls=%async_computation.1 | async-start | bytes 2129920 | tf_op jit(solution)/shard_map/all_gather | solution.py:63
  7.4 26.3 %copy-start.7 = (s32[1,64,8]{1,2,0:T(8,128)S(1)}, s32[1,64,8]{1,2,0:T(8,128)}, u32[]{:S(2)}) copy-start(s32[1,64,8]{1,2,0:T(8,128)} %param.20) | copy-start | bytes 6148
  20.3 13.5 %copy-start.9 = (s32[1,64]{1,0:T(1,128)S(1)}, s32[1,64]{1,0:T(1,128)}, u32[]{:S(2)}) copy-start(s32[1,64]{1,0:T(1,128)} %param.21) | copy-start | bytes 772
  20.3 25.7 %copy-start.8 = (s32[64,8]{0,1:T(8,128)S(1)}, s32[64,8]{0,1:T(8,128)}, u32[]{:S(2)}) copy-start(s32[64,8]{0,1:T(8,128)} %param.14) | copy-start | bytes 6148
  20.3 26.5 %copy-start.6 = (s32[64,16]{0,1:T(8,128)S(1)}, s32[64,16]{0,1:T(8,128)}, u32[]{:S(2)}) copy-start(s32[64,16]{0,1:T(8,128)} %param.22) | copy-start | bytes 12292
  20.3 27.2 %copy-start.4 = (f32[32,2048]{1,0:T(8,128)S(1)}, f32[32,2048]{1,0:T(8,128)}, u32[]{:S(2)}) copy-start(f32[32,2048]{1,0:T(8,128)} %param.18) | copy-start | bytes 786436
  20.4 105.0 %collective-permute-start = (f32[16,4096]{1,0:T(8,128)S(1)}, f32[16,4096]{1,0:T(8,128)}, u32[]{:S(2)}, u32[]{:S(2)}) collective-permute-start(f32[16,4096]{1,0:T(8,128)S(1)} %reshape.187), channel_id=1, source_target_pairs={{0,4},{4,8},{8,12},{12,16},{16,20},{20,24},{24,28},{28,32},{32,36}... | collective-permute-start | bytes 786440 | tf_op jit(solution)/shard_map/ppermute | solution.py:17
  22.4 103.1 %collective-permute-start.1 = (f32[16,4096]{1,0:T(8,128)S(1)}, f32[16,4096]{1,0:T(8,128)}, u32[]{:S(2)}, u32[]{:S(2)}) collective-permute-start(f32[16,4096]{1,0:T(8,128)S(1)} %reshape.187), channel_id=1, source_target_pairs={{4,0},{8,4},{12,8},{16,12},{20,16},{24,20},{28,24},{32,28},{36,32}... | collective-permute-start | bytes 786440 | tf_op jit(solution)/shard_map/ppermute | solution.py:18
  34.6 81.9 %all-to-all-start = ((s32[64,1,8]{2,1,0:T(1,128)}), s32[64,1,8]{2,1,0:T(1,128)}, u32[]{:S(2)}, u32[]{:S(2)}) async-start(s32[64,1,8]{2,1,0:T(1,128)} %compare_select_fusion), calls=%async_computation | async-start | bytes 65536 | tf_op jit(solution)/shard_map/all_to_all | solution.py:60
  46.0 138.0 %all-reduce.3.cloned.1.call-start = ((), (), s32[]{:S(2)}) async-start(), calls=%async_computation.2 | async-start | bytes 524288
  47.9 50.2 %copy-start.2 = (f32[2,64,4096]{2,1,0:T(8,128)S(1)}, f32[2,64,4096]{2,1,0:T(8,128)}, u32[]{:S(2)}) copy-start(f32[2,64,4096]{2,1,0:T(8,128)} %param.15) | copy-start | bytes 6291460
  101.1 11.4 %copy-start.5 = (f32[32,2048]{1,0:T(8,128)S(1)}, f32[32,2048]{1,0:T(8,128)}, u32[]{:S(2)}) copy-start(f32[32,2048]{1,0:T(8,128)} %param.19) | copy-start | bytes 786436
  101.1 12.8 %copy-start.3 = (f32[32,4096]{1,0:T(8,128)S(1)}, f32[32,4096]{1,0:T(8,128)}, u32[]{:S(2)}) copy-start(f32[32,4096]{1,0:T(8,128)} %param.17) | copy-start | bytes 1572868
  112.6 2.8 %copy-start.10 = (u32[256]{0:T(256)S(1)}, u32[256]{0:T(256)}, u32[]{:S(2)}) copy-start(u32[256]{0:T(256)} %constant.40) | copy-start | bytes 3076
  143.6 19.3 %copy-start.1 = (f32[32,64,32]{2,1,0:T(8,128)S(1)}, f32[32,64,32]{2,1,0:T(8,128)}, u32[]{:S(2)}) copy-start(f32[32,64,32]{2,1,0:T(8,128)} %reshape.133) | copy-start | bytes 786436
  162.8 1.5 copy-start
Sparse Core Ops, SparseCore 0:
  33.8 77.8 all-gather.2
Sparse Core Ops, SparseCore 1:
  138.3 45.6 all-reduce.2
where the time goes:
time: 194 us; the launch traced here: 193 us
  blocking collectives  56.7 us (29%)
  local copies, waits for them, and re-layouts  41.5 us (21%)
  matrix products  35.1 us (18%)
  starting transfers between devices  19.1 us (10%)
  waiting for transfers between devices  18 us (9%)
  between operations  15.7 us (8%)
  other arithmetic  6.77 us (3%)
    all_gather x1, blocking collectives, local(): all_parents = lax.all_gather(parents, 'leaf', axis=0, tiled=True)  43.8 us
    dot_general x7, matrix products, contract(): return jnp.einsum(pattern, left, right, precision=lax.Precision.HIGHEST)  35.1 us
    unnamed x3, waiting for transfers between devices  18 us
    all_gather x1, blocking collectives, local(): source = lax.all_gather(points_x, 'vec', axis=0, tiled=True)  12.9 us
    reshape x1, local copies, waits for them, and re-layouts, local(): leaf_coupling.reshape(far_count, RANK, leaf_count, RANK)  11.4 us
    all_to_all x1, starting transfers between devices, local(): lax.all_to_all(sender_ids, 'leaf', split_axis=0, concat_axis=0, tiled=True)  11.4 us
    gather x1, local copies, waits for them, and re-layouts, local(): wanted = received_ids[recv_slot]  6.86 us
    ppermute x1, starting transfers between devices, padded_2(): after = lax.ppermute(leading, axis, down)  5.75 us
  transfers between devices with their start and end apart: 5, of which 1 were waited for; matrix products, arithmetic and copies ran while one was open for 42% of the time, Pallas kernels for 0%

commit v1 on v0

v1 whole, which is shorter than its diff:
```python
import jax
import jax.numpy as jnp
from jax import lax
from jax.experimental import pallas as pl
from jax.experimental.pallas import tpu as pltpu
from jax.sharding import PartitionSpec as P

PTS = 64
RANK = 32
GROUP = 8
LANES = 128
F32 = jnp.float32
BF16 = jnp.bfloat16


def iota(shape, dim):
    return lax.broadcasted_iota(jnp.int32, shape, dim)


def split(value):
    high = value.astype(BF16)
    return high, (value - high.astype(F32)).astype(BF16)


NN = (((1,), (0,)), ((), ()))
NT = (((1,), (1,)), ((), ()))


def mxu(left, right, dims=NN):
    return lax.dot_general(left, right, dims, preferred_element_type=F32)


def dot3(left, right, dims=NN):
    rows = left.shape[0]
    left_high, left_low = split(left)
    right_high, right_low = split(right)
    both = mxu(jnp.concatenate([left_high, left_low], axis=0), right_high, dims)
    return both[:rows] + both[rows:] + mxu(left_high, right_low, dims)


def fold(value):
    value = value[:, :LANES] + value[:, LANES:]
    value = value + pltpu.roll(value, 64, 1)
    return value + pltpu.roll(value, 32, 1)


def pick_rows(rows_of, table_high, table_low):
    count, columns = rows_of.shape
    entries = table_high.shape[0]
    lane = iota((count, entries), 1)
    hot = jnp.concatenate(
        [
            jnp.where(rows_of[:, j : j + 1] == lane, 1.0, 0.0).astype(BF16)
            for j in range(columns)
        ],
        axis=0,
    )
    got = mxu(hot, jnp.concatenate([table_high, table_low], axis=1))
    return got[:, :LANES] + got[:, LANES:]


def by_column(tiles, columns):
    block = iota((GROUP, LANES), 1) // RANK
    per = LANES // RANK
    rows = []
    for c in range(columns):
        pieces = []
        for first in range(0, len(tiles), per):
            piece = None
            for k in range(per):
                shift = ((k - c) * RANK) % LANES
                tile = tiles[first + k]
                moved = pltpu.roll(tile, shift, 1) if shift else tile
                piece = moved if piece is None else jnp.where(block == k, moved, piece)
            pieces.append(piece)
        rows.append(jnp.concatenate(pieces, axis=1))
    return jnp.concatenate(rows, axis=0)


def up_kernel(x_ref, basis_ref, up_ref, leaves_ref, counts_ref, send_ref):
    columns = x_ref.shape[0]
    leaf_count = x_ref.shape[1] // PTS
    peers, slots = leaves_ref.shape
    wide = GROUP * PTS
    own = iota((GROUP, wide), 1) // PTS == iota((GROUP, wide), 0)
    lane_block = iota((GROUP, LANES), 1) // RANK
    diagonal = iota((columns * GROUP, GROUP * RANK), 1) // RANK == (
        iota((columns * GROUP, GROUP * RANK), 0) % GROUP
    )
    skeleton, parents = [], []
    for q in range(leaf_count // GROUP):
        x = x_ref[:, q * wide : (q + 1) * wide]
        spread = jnp.concatenate(
            [jnp.where(own, x[c : c + 1], 0.0) for c in range(columns)], axis=0
        )
        tile = dot3(spread, basis_ref[:, q * wide : (q + 1) * wide], NT)
        skeleton.append(
            jnp.concatenate(
                [tile[c * GROUP : (c + 1) * GROUP] for c in range(columns)], axis=1
            )
        )
        narrow = GROUP * RANK
        lifted = dot3(tile, up_ref[:, q * narrow : (q + 1) * narrow])
        lifted = fold(jnp.where(diagonal, lifted, 0.0))
        total = None
        for c in range(columns):
            part = jnp.where(lane_block == c, lifted[c * GROUP : (c + 1) * GROUP], 0.0)
            total = part if total is None else total + part
        parents.append(jnp.sum(total, axis=0, keepdims=True))
    skeleton = jnp.concatenate(skeleton, axis=0)
    parents = jnp.concatenate(parents, axis=0)

    counts = jnp.broadcast_to(counts_ref[...].astype(F32), (peers, peers))
    square = iota((peers, peers), 0) == iota((peers, peers), 1)
    count_column = jnp.sum(jnp.where(square, counts, 0.0), axis=1, keepdims=True)
    wanted = jnp.where(
        iota((peers, slots), 1).astype(F32) < count_column, leaves_ref[...].astype(F32), -1.0
    )
    rows = peers * slots
    expand = jnp.where(iota((rows, peers), 0) // slots == iota((rows, peers), 1), 1.0, 0.0)
    wanted = mxu(expand.astype(BF16), wanted.astype(BF16))
    wanted = jnp.sum(
        jnp.where(iota((rows, slots), 0) % slots == iota((rows, slots), 1), wanted, 0.0),
        axis=1,
        keepdims=True,
    )
    hot = jnp.where(wanted == iota((rows, leaf_count), 1).astype(F32), 1.0, 0.0).astype(BF16)
    high, low = split(skeleton)
    got = mxu(hot, jnp.concatenate([high, low], axis=1))
    got = got[:, :LANES] + got[:, LANES:]
    send_ref[:, :slots, :] = got.reshape(peers, slots, LANES)
    par_count = parents.shape[0]
    send_ref[:, slots:, :] = jnp.broadcast_to(parents[None], (peers, par_count, LANES))


def near_kernel(list_ref, own_ref, left_ref, right_ref, blocks_ref, *rest):
    outs, table = rest[:-1], rest[-1]
    total_columns, points = own_ref.shape
    leaf_count = points // PTS
    share = blocks_ref.shape[0]
    columns = total_columns // len(outs)
    base = (lax.axis_index("leaf") - 1) * leaf_count
    first = lax.axis_index("vec") * share
    for place, ref in enumerate((left_ref, own_ref, right_ref)):
        for b in range(points // LANES):
            tile = ref[:, b * LANES : (b + 1) * LANES]
            at = place * (points // LANES) + b
            table[0, at] = tile
            table[1, at] = pltpu.roll(tile, PTS, 1)
    lower = iota((total_columns, LANES), 1) < PTS
    per = 4
    for g in range(leaf_count // per):
        tiles = []
        for i in range(per):
            t = g * per + i
            one = list_ref[t, first] - base
            two = list_ref[t, first + 1] - base
            tiles.append(
                jnp.where(
                    lower, table[one % 2, one // 2], table[1 - two % 2, two // 2]
                )
            )
        sources = jnp.concatenate(tiles, axis=0)
        lanes = slice(g * per * PTS, (g + 1) * per * PTS)
        block = blocks_ref[:, :, lanes].reshape(share * PTS, per * PTS)
        value = dot3(sources, block)
        for h in range(per // 2):
            at = 2 * h * total_columns
            cut = slice(h * LANES, (h + 1) * LANES)
            result = jnp.where(
                lower,
                value[at : at + total_columns, cut],
                value[at + total_columns : at + 2 * total_columns, cut],
            )
            place = slice((g * per // 2 + h) * LANES, (g * per // 2 + h + 1) * LANES)
            for s, out in enumerate(outs):
                out[:, place] = result[s * columns : (s + 1) * columns]


def far_kernel(
    recv_ref, slot_ref, top_ref, coupling_ref, top_coupling_ref, down_ref, basis_ref, out_ref
):
    columns, points = out_ref.shape
    leaf_count = points // PTS
    peers = recv_ref.shape[0]
    par_count = leaf_count // GROUP
    slots = recv_ref.shape[1] - par_count
    far_count = coupling_ref.shape[0]
    top_count = top_coupling_ref.shape[0]
    narrow, wide = GROUP * RANK, GROUP * PTS
    rows = columns * GROUP
    diagonal = iota((rows, narrow), 1) // RANK == iota((rows, narrow), 0) % GROUP
    diagonal_out = iota((rows, wide), 1) // PTS == iota((rows, wide), 0) % GROUP

    tops = recv_ref[:, slots:, :].reshape(peers * par_count, LANES)
    got = pick_rows(top_ref[...], *split(tops))
    field = dot3(
        by_column([got[j * GROUP : (j + 1) * GROUP] for j in range(top_count)], columns),
        top_coupling_ref[...].reshape(top_count * RANK, narrow),
    )
    field = fold(jnp.where(diagonal, field, 0.0))[:, :RANK]
    lowered = dot3(field, down_ref[...])

    tiles = recv_ref[:, :slots, :].reshape(peers * slots, LANES)
    got = pick_rows(slot_ref[...], *split(tiles))
    for g in range(par_count):
        sources = by_column(
            [
                got[j * leaf_count + g * GROUP : j * leaf_count + (g + 1) * GROUP]
                for j in range(far_count)
            ],
            columns,
        )
        lanes = slice(g * narrow, (g + 1) * narrow)
        value = dot3(sources, coupling_ref[:, :, lanes].reshape(far_count * RANK, narrow))
        value = value + jnp.concatenate(
            [
                jnp.broadcast_to(
                    lowered[c * GROUP + g : c * GROUP + g + 1, lanes], (GROUP, narrow)
                )
                for c in range(columns)
            ],
            axis=0,
        )
        local_field = fold(jnp.where(diagonal, value, 0.0))[:, :RANK]
        value = dot3(local_field, basis_ref[:, g * wide : (g + 1) * wide])
        value = jnp.where(diagonal_out, value, 0.0)
        out_ref[:, g * wide : (g + 1) * wide] = jnp.sum(
            value.reshape(columns, GROUP, wide), axis=1
        )


VMEM = pl.BlockSpec(memory_space=pltpu.VMEM)
SMEM = pl.BlockSpec(memory_space=pltpu.SMEM)
PARAMS = pltpu.CompilerParams(vmem_limit_bytes=40 * 1024 * 1024)


def local(
    points_x,
    near_list,
    near_blocks,
    leaf_basis,
    out_basis,
    up_transfer,
    down_transfer,
    send_leaves,
    send_counts,
    recv_slot,
    leaf_coupling,
    top_list,
    top_coupling,
):
    columns, points = points_x.shape
    leaf_count = near_list.shape[0]
    par_count = top_list.shape[0]
    peers, slots = send_leaves.shape[1:]
    groups = lax.axis_size("vec")
    ring = lax.axis_size("leaf")

    others = [
        lax.ppermute(points_x, "vec", [(i, (i + s) % groups) for i in range(groups)])
        for s in range(1, groups)
    ]
    send = pl.pallas_call(
        up_kernel,
        name="up",
        out_shape=jax.ShapeDtypeStruct((peers, slots + par_count, LANES), F32),
        in_specs=[VMEM] * 5,
        out_specs=VMEM,
        compiler_params=PARAMS,
    )(points_x, leaf_basis, up_transfer, send_leaves[0], send_counts)
    every = jnp.concatenate([points_x] + others, axis=0)
    left = lax.ppermute(every, "leaf", [(i, (i + 1) % ring) for i in range(ring)])
    right = lax.ppermute(every, "leaf", [((i + 1) % ring, i) for i in range(ring)])
    recv = lax.all_to_all(send, "leaf", split_axis=0, concat_axis=0, tiled=True)
    partial = pl.pallas_call(
        near_kernel,
        name="near",
        out_shape=[jax.ShapeDtypeStruct((columns, points), F32)] * groups,
        in_specs=[SMEM] + [VMEM] * 4,
        out_specs=[VMEM] * groups,
        scratch_shapes=[pltpu.VMEM((2, 3 * points // LANES, columns * groups, LANES), F32)],
        compiler_params=PARAMS,
        cost_estimate=pl.CostEstimate(
            flops=2 * near_blocks.size * columns * groups,
            bytes_accessed=4 * near_blocks.size,
            transcendentals=0,
        ),
    )(near_list, every, left, right, near_blocks)
    parts = [partial[0]] + [
        lax.ppermute(partial[s], "vec", [(i, (i - s) % groups) for i in range(groups)])
        for s in range(1, groups)
    ]
    far = pl.pallas_call(
        far_kernel,
        name="far",
        out_shape=jax.ShapeDtypeStruct((columns, points), F32),
        in_specs=[VMEM] * 7,
        out_specs=VMEM,
        compiler_params=PARAMS,
    )(recv, recv_slot, top_list, leaf_coupling, top_coupling, down_transfer, out_basis)
    return far + sum(parts[1:], parts[0])


def solution(mesh):
    placed = (
        P("vec", "leaf"),
        P("leaf", None),
        P("vec", None, "leaf"),
        P(None, "leaf"),
        P(None, "leaf"),
        P(None, "leaf"),
        P(None, "leaf"),
        P("leaf", None, None),
        P("leaf", None),
        P("leaf", None),
        P(None, None, "leaf"),
        P("leaf", None),
        P(None, None, "leaf"),
    )
    return jax.shard_map(
        local, mesh=mesh, in_specs=placed, out_specs=P("vec", "leaf"), check_vma=False
    )
```

time: 194 us -> 57.2 us (0.29)
  the two profiles are of different devices: /device:TPU:8 before, /device:TPU:2 now
where the time goes in v1:
time: 57.2 us; the launch traced here: 56.8 us
  starting transfers between devices  26.8 us (47%)
  Pallas kernels  10.5 us (18%)
  local copies, waits for them, and re-layouts  9.35 us (16%)
  waiting for transfers between devices  8.46 us (15%)
  other arithmetic  1.57 us (3%)
    all_to_all x1, starting transfers between devices, local(): recv = lax.all_to_all(send, 'leaf', split_axis=0, concat_axis=0, tiled=True)  12.1 us
    unnamed x25, local copies, waits for them, and re-layouts  9.35 us
    ppermute x1, waiting for transfers between devices, local(): lax.ppermute(every, 'leaf', [(i, (i + 1) % ring) for i in range(ring)])  5.75 us
    ppermute x1, starting transfers between devices, local(): lax.ppermute(every, 'leaf', [((i + 1) % ring, i) for i in range(ring)])  5.05 us
    ppermute x3, starting transfers between devices, local(): lax.ppermute(points_x, 'vec', [(i, (i + s) % groups) for i in range(group...  4.83 us
    pallas_call x1, Pallas kernels, local(): pl.pallas_call(far_kernel, name='far', out_shape=jax.ShapeDtypeStruct((co...  4.78 us
    ppermute x3, starting transfers between devices, local(): lax.ppermute(partial[s], 'vec', [(i, (i - s) % groups) for i in range(gro...  4.75 us
    pallas_call x1, Pallas kernels, local(): pl.pallas_call(near_kernel, name='near', out_shape=[jax.ShapeDtypeStruct(...  3.08 us
  transfers between devices with their start and end apart: 9, of which 3 were waited for; matrix products, arithmetic and copies ran while one was open for 3% of the time, Pallas kernels for 14%

profile of v1, /device:TPU:2, one launch (start us, length us, event | category | flops | bytes accessed | tf_op | source)
XLA Modules:
  0.0 56.8 jit_solution(17479513725468783360)
XLA Ops:
  0.0 0.0 copy-start.1
  0.0 0.9 %copy.14 = s32[1,64,8]{2,1,0:T(8,128)S(1)} copy(s32[1,64,8]{1,2,0:T(8,128)} %param.20) | data formatting | bytes 4096 | tf_op args[7]
  0.9 0.0 copy-start.2
  0.9 1.0 %copy-done.2 = f32[32,4096]{1,0:T(8,128)S(1)} copy-done((f32[32,4096]{1,0:T(8,128)S(1)}, f32[32,4096]{1,0:T(8,128)}, u32[]{:S(2)}) %copy-start.2) | copy-done | bytes 524312
  2.0 0.0 copy-start.4
  2.0 0.9 %copy-done.4 = f32[32,2048]{1,0:T(8,128)S(1)} copy-done((f32[32,2048]{1,0:T(8,128)S(1)}, f32[32,2048]{1,0:T(8,128)}, u32[]{:S(2)}) %copy-start.4) | copy-done | bytes 262168
  2.9 0.0 copy-start.7
  2.9 0.8 %copy-done.7 = f32[4,4096]{1,0:T(4,128)S(1)} copy-done((f32[4,4096]{1,0:T(4,128)S(1)}, f32[4,4096]{1,0:T(4,128)}, u32[]{:S(2)}) %copy-start.7) | copy-done | bytes 65560
  3.8 0.0 copy-start.9
  3.8 0.7 %copy-done.9 = s32[1,64]{1,0:T(1,128)S(1)} copy-done((s32[1,64]{1,0:T(1,128)S(1)}, s32[1,64]{1,0:T(1,128)}, u32[]{:S(2)}) %copy-start.9) | copy-done | bytes 280
  4.4 0.0 copy-start.10
  4.4 0.0 copy-start.3
  4.4 0.0 copy-start.8
  4.4 2.6 %up.1 = f32[64,16,128]{2,1,0:T(8,128)} custom-call(f32[4,4096]{1,0:T(4,128)S(1)} %copy-done.7, f32[32,4096]{1,0:T(8,128)S(1)} %copy-done.2, f32[32,2048]{1,0:T(8,128)S(1)} %copy-done.4, s32[64,8]{1,0:T(8,128)S(1)} %bitcast.1, s32[1,64]{1,0:T(1,128)S(1)} %copy-done.9), custom_call_target="tpu_custom_call" | custom-call | tf_op jit(solution)/shard_map/up/pallas_call | solution.py:264
  7.0 12.1 %all-to-all-start = ((f32[64,16,128]{2,1,0:T(8,128)}), f32[64,16,128]{2,1,0:T(8,128)S(1)}, u32[]{:S(2)}, u32[]{:S(2)}) async-start(f32[64,16,128]{2,1,0:T(8,128)} %up.1), calls=%async_computation | async-start | bytes 1048576 | tf_op jit(solution)/shard_map/all_to_all | solution.py:275
  19.1 0.6 %collective-permute-start.2 = (f32[4,4096]{1,0:T(4,128)}, f32[4,4096]{1,0:T(4,128)S(1)}, u32[]{:S(2)}, u32[]{:S(2)}) collective-permute-start(f32[4,4096]{1,0:T(4,128)} %x_ref.1), channel_id=1, source_target_pairs={{0,3},{1,0},{2,1},{3,2},{4,7},{5,4},{6,5},{7,6},{8,11},{9,8},{10,9... | collective-permute-start | bytes 196616 | tf_op jit(solution)/shard_map/ppermute | solution.py:261
  19.8 2.4 %collective-permute-start.1 = (f32[4,4096]{1,0:T(4,128)}, f32[4,4096]{1,0:T(4,128)S(1)}, u32[]{:S(2)}, u32[]{:S(2)}) collective-permute-start(f32[4,4096]{1,0:T(4,128)} %x_ref.1), channel_id=1, source_target_pairs={{0,2},{1,3},{2,0},{3,1},{4,6},{5,7},{6,4},{7,5},{8,10},{9,11},{10,... | collective-permute-start | bytes 196616 | tf_op jit(solution)/shard_map/ppermute | solution.py:261
  22.2 1.8 %collective-permute-start = (f32[4,4096]{1,0:T(4,128)}, f32[4,4096]{1,0:T(4,128)S(1)}, u32[]{:S(2)}, u32[]{:S(2)}) collective-permute-start(f32[4,4096]{1,0:T(4,128)} %x_ref.1), channel_id=1, source_target_pairs={{0,1},{1,2},{2,3},{3,0},{4,5},{5,6},{6,7},{7,4},{8,9},{9,10},{10,1... | collective-permute-start | bytes 196616 | tf_op jit(solution)/shard_map/ppermute | solution.py:261
  24.0 0.0 collective-permute-done.2
  24.0 2.0 %collective-permute-done.1 = f32[4,4096]{1,0:T(4,128)S(1)} collective-permute-done((f32[4,4096]{1,0:T(4,128)}, f32[4,4096]{1,0:T(4,128)S(1)}, u32[]{:S(2)}, u32[]{:S(2)}) %collective-permute-start.1) | collective-permute-done | bytes 65568 | tf_op jit(solution)/shard_map/ppermute | solution.py:261
  25.9 0.7 %collective-permute-done = f32[4,4096]{1,0:T(4,128)S(1)} collective-permute-done((f32[4,4096]{1,0:T(4,128)}, f32[4,4096]{1,0:T(4,128)S(1)}, u32[]{:S(2)}, u32[]{:S(2)}) %collective-permute-start) | collective-permute-done | bytes 65568 | tf_op jit(solution)/shard_map/ppermute | solution.py:261
  26.7 0.9 %pad_maximum_fusion.own_ref = f32[16,4096]{1,0:T(8,128)S(1)} fusion(f32[4,4096]{1,0:T(4,128)S(1)} %collective-permute-done.2, f32[4,4096]{1,0:T(4,128)S(1)} %collective-permute-done.1, f32[4,4096]{1,0:T(4,128)S(1)} %collective-permute-done, f32[4,4096]{1,0:T(4,128)} %x_ref.1), kind=kLoop, calls=%fused_computation | loop fusion | flops 196608 | bytes 524288 | tf_op jit(solution)/shard_map/concatenate | solution.py:272
  27.6 0.1 collective-permute-start.3
  27.7 5.1 %collective-permute-start.4 = (f32[16,4096]{1,0:T(8,128)S(1)}, f32[16,4096]{1,0:T(8,128)}, u32[]{:S(2)}, u32[]{:S(2)}) collective-permute-start(f32[16,4096]{1,0:T(8,128)S(1)} %pad_maximum_fusion.own_ref), channel_id=1, source_target_pairs={{4,0},{8,4},{12,8},{16,12},{20,16},{24,20},{28,24},{32,28},{36,32}... | collective-permute-start | bytes 786440 | tf_op jit(solution)/shard_map/ppermute | solution.py:274
  32.7 0.8 %copy.16.list_ref = s32[64,8]{1,0:T(8,128)S(1)} copy(s32[64,8]{0,1:T(8,128)} %param.14) | data formatting | bytes 4096 | tf_op args[1]
  33.5 5.7 %collective-permute-done.3.left_ref = f32[16,4096]{1,0:T(8,128)} collective-permute-done((f32[16,4096]{1,0:T(8,128)S(1)}, f32[16,4096]{1,0:T(8,128)}, u32[]{:S(2)}, u32[]{:S(2)}) %collective-permute-start.3) | collective-permute-done | bytes 262176 | tf_op jit(solution)/shard_map/ppermute | solution.py:273
  39.2 0.0 collective-permute-done.4.right_ref
  39.3 0.0 copy-done.1
  39.3 3.1 %near.1 = (f32[4,4096]{1,0:T(4,128)S(1)}, f32[4,4096]{1,0:T(4,128)}, f32[4,4096]{1,0:T(4,128)}, f32[4,4096]{1,0:T(4,128)}) custom-call(s32[64,8]{1,0:T(8,128)S(1)} %copy.16.list_ref, f32[16,4096]{1,0:T(8,128)S(1)} %pad_maximum_fusion.own_ref, f32[16,4096]{1,0:T(8,128)} %collective-permute-done.3.left_ref, f32[16,4096]{1,0:T(8,128)} %collective-permute-done.4.right_ref, ...), custom_call_target="tpu_custom_call" | custom-call | flops 16777216 | bytes 2097152 | tf_op jit(solution)/shard_map/near/pallas_call | solution.py:276
  42.3 1.5 %collective-permute-start.7 = (f32[4,4096]{1,0:T(4,128)}, f32[4,4096]{1,0:T(4,128)S(1)}, u32[]{:S(2)}, u32[]{:S(2)}) collective-permute-start(f32[4,4096]{1,0:T(4,128)} %get-tuple-element.12), channel_id=1, source_target_pairs={{0,1},{1,2},{2,3},{3,0},{4,5},{5,6},{6,7},{7,4},{8,9},{9,10},{10,1... | collective-permute-start | bytes 196616 | tf_op jit(solution)/shard_map/ppermute | solution.py:291
  43.8 1.6 %collective-permute-start.6 = (f32[4,4096]{1,0:T(4,128)}, f32[4,4096]{1,0:T(4,128)S(1)}, u32[]{:S(2)}, u32[]{:S(2)}) collective-permute-start(f32[4,4096]{1,0:T(4,128)} %get-tuple-element.11), channel_id=1, source_target_pairs={{0,2},{1,3},{2,0},{3,1},{4,6},{5,7},{6,4},{7,5},{8,10},{9,11},{10,... | collective-permute-start | bytes 196616 | tf_op jit(solution)/shard_map/ppermute | solution.py:291
  45.4 1.7 %collective-permute-start.5 = (f32[4,4096]{1,0:T(4,128)}, f32[4,4096]{1,0:T(4,128)S(1)}, u32[]{:S(2)}, u32[]{:S(2)}) collective-permute-start(f32[4,4096]{1,0:T(4,128)} %get-tuple-element.10), channel_id=1, source_target_pairs={{0,3},{1,0},{2,1},{3,2},{4,7},{5,4},{6,5},{7,6},{8,11},{9,8},{10,9... | collective-permute-start | bytes 196616 | tf_op jit(solution)/shard_map/ppermute | solution.py:291
  47.1 0.0 copy-done.10
  47.1 0.1 copy.15.slot_ref
  47.2 0.0 all-to-all-done.recv_ref
  47.2 0.0 copy-done.3
  47.2 0.0 copy-done.8
  47.2 0.0 copy-start
  47.2 2.2 %copy-done = f32[16,32,2048]{2,1,0:T(8,128)S(1)} copy-done((f32[16,32,2048]{2,1,0:T(8,128)S(1)}, f32[16,32,2048]{2,1,0:T(8,128)}, u32[]{:S(2)}) %copy-start) | copy-done | bytes 4194328
  49.4 0.0 copy-start.5
  49.4 0.9 %copy-done.5 = f32[8,32,256]{2,1,0:T(8,128)S(1)} copy-done((f32[8,32,256]{2,1,0:T(8,128)S(1)}, f32[8,32,256]{2,1,0:T(8,128)}, u32[]{:S(2)}) %copy-start.5) | copy-done | bytes 262168
  50.3 0.0 copy-start.6
  50.3 0.9 %copy-done.6 = f32[32,2048]{1,0:T(8,128)S(1)} copy-done((f32[32,2048]{1,0:T(8,128)S(1)}, f32[32,2048]{1,0:T(8,128)}, u32[]{:S(2)}) %copy-start.6) | copy-done | bytes 262168
  51.3 4.8 %far.1 = f32[4,4096]{1,0:T(4,128)S(1)} custom-call(f32[64,16,128]{2,1,0:T(8,128)S(1)} %all-to-all-done.recv_ref, s32[64,16]{1,0:T(8,128)S(1)} %copy.15.slot_ref, s32[8,8]{1,0:T(8,128)S(1)} %copy-done.8, f32[16,32,2048]{2,1,0:T(8,128)S(1)} %copy-done, f32[8,32,256]{2,1,0:T(8,128)S(1)} %copy-done.5, f32[32,2048]{1,0:T(8,128)S(1)} %copy-done.6, ...), custom_call_target="tpu_custom_call" | custom-call | tf_op jit(solution)/shard_map/far/pallas_call | solution.py:294
  56.1 0.0 collective-permute-done.7
  56.1 0.0 collective-permute-done.6
  56.1 0.0 collective-permute-done.5
  56.1 0.7 %add_add_fusion = f32[4,4096]{1,0:T(4,128)} fusion(f32[4,4096]{1,0:T(4,128)S(1)} %far.1, f32[4,4096]{1,0:T(4,128)S(1)} %collective-permute-done.7, f32[4,4096]{1,0:T(4,128)S(1)} %collective-permute-done.6, f32[4,4096]{1,0:T(4,128)S(1)} %get-tuple-element.9, f32[4,4096]{1,0:T(4,128)S(1)} %collective-permute-done.5), kind=kLoop, calls=%fused_computation.1 | loop fusion | flops 65536 | bytes 393216 | tf_op jit(solution)/shard_map/add | solution.py:302
Async XLA Ops:
  0.0 39.3 %copy-start.1 = (f32[2,64,4096]{2,1,0:T(8,128)S(1)}, f32[2,64,4096]{2,1,0:T(8,128)}, u32[]{:S(2)}) copy-start(f32[2,64,4096]{2,1,0:T(8,128)} %blocks_ref.1) | copy-start | bytes 6291460
  0.9 1.0 %copy-start.2 = (f32[32,4096]{1,0:T(8,128)S(1)}, f32[32,4096]{1,0:T(8,128)}, u32[]{:S(2)}) copy-start(f32[32,4096]{1,0:T(8,128)} %basis_ref.2) | copy-start | bytes 1572868
  2.0 0.9 %copy-start.4 = (f32[32,2048]{1,0:T(8,128)S(1)}, f32[32,2048]{1,0:T(8,128)}, u32[]{:S(2)}) copy-start(f32[32,2048]{1,0:T(8,128)} %up_ref.1) | copy-start | bytes 786436
  2.9 0.8 %copy-start.7 = (f32[4,4096]{1,0:T(4,128)S(1)}, f32[4,4096]{1,0:T(4,128)}, u32[]{:S(2)}) copy-start(f32[4,4096]{1,0:T(4,128)} %x_ref.1) | copy-start | bytes 196612
  3.8 0.7 %copy-start.9 = (s32[1,64]{1,0:T(1,128)S(1)}, s32[1,64]{1,0:T(1,128)}, u32[]{:S(2)}) copy-start(s32[1,64]{1,0:T(1,128)} %counts_ref.1) | copy-start | bytes 772
  4.4 42.7 %copy-start.10 = (s32[64,16]{0,1:T(8,128)S(1)}, s32[64,16]{0,1:T(8,128)}, u32[]{:S(2)}) copy-start(s32[64,16]{0,1:T(8,128)} %param.22) | copy-start | bytes 12292
  4.4 42.8 %copy-start.3 = (f32[32,4096]{1,0:T(8,128)S(1)}, f32[32,4096]{1,0:T(8,128)}, u32[]{:S(2)}) copy-start(f32[32,4096]{1,0:T(8,128)} %basis_ref.3) | copy-start | bytes 1572868
  4.4 42.8 %copy-start.8 = (s32[8,8]{1,0:T(8,128)S(1)}, s32[8,8]{1,0:T(8,128)}, u32[]{:S(2)}) copy-start(s32[8,8]{1,0:T(8,128)} %top_ref.1) | copy-start | bytes 772
  7.0 40.1 %all-to-all-start = ((f32[64,16,128]{2,1,0:T(8,128)}), f32[64,16,128]{2,1,0:T(8,128)S(1)}, u32[]{:S(2)}, u32[]{:S(2)}) async-start(f32[64,16,128]{2,1,0:T(8,128)} %up.1), calls=%async_computation | async-start | bytes 1048576 | tf_op jit(solution)/shard_map/all_to_all | solution.py:275
  19.1 4.8 %collective-permute-start.2 = (f32[4,4096]{1,0:T(4,128)}, f32[4,4096]{1,0:T(4,128)S(1)}, u32[]{:S(2)}, u32[]{:S(2)}) collective-permute-start(f32[4,4096]{1,0:T(4,128)} %x_ref.1), channel_id=1, source_target_pairs={{0,3},{1,0},{2,1},{3,2},{4,7},{5,4},{6,5},{7,6},{8,11},{9,8},{10,9... | collective-permute-start | bytes 196616 | tf_op jit(solution)/shard_map/ppermute | solution.py:261
  19.8 6.2 %collective-permute-start.1 = (f32[4,4096]{1,0:T(4,128)}, f32[4,4096]{1,0:T(4,128)S(1)}, u32[]{:S(2)}, u32[]{:S(2)}) collective-permute-start(f32[4,4096]{1,0:T(4,128)} %x_ref.1), channel_id=1, source_target_pairs={{0,2},{1,3},{2,0},{3,1},{4,6},{5,7},{6,4},{7,5},{8,10},{9,11},{10,... | collective-permute-start | bytes 196616 | tf_op jit(solution)/shard_map/ppermute | solution.py:261
  22.2 4.5 %collective-permute-start = (f32[4,4096]{1,0:T(4,128)}, f32[4,4096]{1,0:T(4,128)S(1)}, u32[]{:S(2)}, u32[]{:S(2)}) collective-permute-start(f32[4,4096]{1,0:T(4,128)} %x_ref.1), channel_id=1, source_target_pairs={{0,1},{1,2},{2,3},{3,0},{4,5},{5,6},{6,7},{7,4},{8,9},{9,10},{10,1... | collective-permute-start | bytes 196616 | tf_op jit(solution)/shard_map/ppermute | solution.py:261
  27.6 11.7 %collective-permute-start.3 = (f32[16,4096]{1,0:T(8,128)S(1)}, f32[16,4096]{1,0:T(8,128)}, u32[]{:S(2)}, u32[]{:S(2)}) collective-permute-start(f32[16,4096]{1,0:T(8,128)S(1)} %pad_maximum_fusion.own_ref), channel_id=1, source_target_pairs={{0,4},{4,8},{8,12},{12,16},{16,20},{20,24},{24,28},{28,32},{32,36}... | collective-permute-start | bytes 786440 | tf_op jit(solution)/shard_map/ppermute | solution.py:273
  27.7 11.6 %collective-permute-start.4 = (f32[16,4096]{1,0:T(8,128)S(1)}, f32[16,4096]{1,0:T(8,128)}, u32[]{:S(2)}, u32[]{:S(2)}) collective-permute-start(f32[16,4096]{1,0:T(8,128)S(1)} %pad_maximum_fusion.own_ref), channel_id=1, source_target_pairs={{4,0},{8,4},{12,8},{16,12},{20,16},{24,20},{28,24},{32,28},{36,32}... | collective-permute-start | bytes 786440 | tf_op jit(solution)/shard_map/ppermute | solution.py:274
  42.3 13.7 %collective-permute-start.7 = (f32[4,4096]{1,0:T(4,128)}, f32[4,4096]{1,0:T(4,128)S(1)}, u32[]{:S(2)}, u32[]{:S(2)}) collective-permute-start(f32[4,4096]{1,0:T(4,128)} %get-tuple-element.12), channel_id=1, source_target_pairs={{0,1},{1,2},{2,3},{3,0},{4,5},{5,6},{6,7},{7,4},{8,9},{9,10},{10,1... | collective-permute-start | bytes 196616 | tf_op jit(solution)/shard_map/ppermute | solution.py:291
  43.8 12.3 %collective-permute-start.6 = (f32[4,4096]{1,0:T(4,128)}, f32[4,4096]{1,0:T(4,128)S(1)}, u32[]{:S(2)}, u32[]{:S(2)}) collective-permute-start(f32[4,4096]{1,0:T(4,128)} %get-tuple-element.11), channel_id=1, source_target_pairs={{0,2},{1,3},{2,0},{3,1},{4,6},{5,7},{6,4},{7,5},{8,10},{9,11},{10,... | collective-permute-start | bytes 196616 | tf_op jit(solution)/shard_map/ppermute | solution.py:291
  45.4 10.7 %collective-permute-start.5 = (f32[4,4096]{1,0:T(4,128)}, f32[4,4096]{1,0:T(4,128)S(1)}, u32[]{:S(2)}, u32[]{:S(2)}) collective-permute-start(f32[4,4096]{1,0:T(4,128)} %get-tuple-element.10), channel_id=1, source_target_pairs={{0,3},{1,0},{2,1},{3,2},{4,7},{5,4},{6,5},{7,6},{8,11},{9,8},{10,9... | collective-permute-start | bytes 196616 | tf_op jit(solution)/shard_map/ppermute | solution.py:291
  47.2 2.2 %copy-start = (f32[16,32,2048]{2,1,0:T(8,128)S(1)}, f32[16,32,2048]{2,1,0:T(8,128)}, u32[]{:S(2)}) copy-start(f32[16,32,2048]{2,1,0:T(8,128)} %coupling_ref.1) | copy-start | bytes 12582916
  49.4 0.9 %copy-start.5 = (f32[8,32,256]{2,1,0:T(8,128)S(1)}, f32[8,32,256]{2,1,0:T(8,128)}, u32[]{:S(2)}) copy-start(f32[8,32,256]{2,1,0:T(8,128)} %top_coupling_ref.1) | copy-start | bytes 786436
  50.3 0.9 %copy-start.6 = (f32[32,2048]{1,0:T(8,128)S(1)}, f32[32,2048]{1,0:T(8,128)}, u32[]{:S(2)}) copy-start(f32[32,2048]{1,0:T(8,128)} %down_ref.1) | copy-start | bytes 786436

commit v2 on v1

v2 whole, which is shorter than its diff:
```python
import jax
import jax.numpy as jnp
from jax import lax
from jax.experimental import pallas as pl
from jax.experimental.pallas import tpu as pltpu
from jax.sharding import PartitionSpec as P

PTS = 64
RANK = 32
GROUP = 8
LANES = 128
F32 = jnp.float32
BF16 = jnp.bfloat16


def iota(shape, dim):
    return lax.broadcasted_iota(jnp.int32, shape, dim)


def split(value):
    high = value.astype(BF16)
    return high, (value - high.astype(F32)).astype(BF16)


NN = (((1,), (0,)), ((), ()))
NT = (((1,), (1,)), ((), ()))


def mxu(left, right, dims=NN):
    return lax.dot_general(left, right, dims, preferred_element_type=F32)


def dot3(left, right, dims=NN):
    rows = left.shape[0]
    left_high, left_low = split(left)
    right_high, right_low = right if isinstance(right, tuple) else split(right)
    both = mxu(jnp.concatenate([left_high, left_low], axis=0), right_high, dims)
    return both[:rows] + both[rows:] + mxu(left_high, right_low, dims)


def fold(value):
    value = value[:, :LANES] + value[:, LANES:]
    value = value + pltpu.roll(value, 64, 1)
    return value + pltpu.roll(value, 32, 1)


def hot_rows(rows_of, entries):
    count, columns = rows_of.shape
    lane = iota((count, entries), 1)
    return jnp.concatenate(
        [
            jnp.where(rows_of[:, j : j + 1] == lane, 1.0, 0.0).astype(BF16)
            for j in range(columns)
        ],
        axis=0,
    )


def pick_rows(hot, table):
    got = mxu(hot, jnp.concatenate(split(table), axis=1))
    return got[:, :LANES] + got[:, LANES:]


def by_column(tiles, columns):
    block = iota((GROUP, LANES), 1) // RANK
    per = LANES // RANK
    rows = []
    for c in range(columns):
        pieces = []
        for first in range(0, len(tiles), per):
            piece = None
            for k in range(per):
                shift = ((k - c) * RANK) % LANES
                tile = tiles[first + k]
                moved = pltpu.roll(tile, shift, 1) if shift else tile
                piece = moved if piece is None else jnp.where(block == k, moved, piece)
            pieces.append(piece)
        rows.append(jnp.concatenate(pieces, axis=1))
    return jnp.concatenate(rows, axis=0)


def fetch(sources, targets, sems):
    copies = [
        pltpu.make_async_copy(source, target, sems.at[i])
        for i, (source, target) in enumerate(zip(sources, targets))
    ]
    for copy in copies:
        copy.start()
    return copies


def up_kernel(x_in, basis_in, up_in, leaves_in, counts_in, send_ref, *scratch):
    x_ref, basis_ref, up_ref, leaves_ref, counts_ref, sems = scratch
    for copy in fetch((x_in, basis_in, up_in, leaves_in, counts_in), scratch[:5], sems):
        copy.wait()
    columns = x_ref.shape[0]
    leaf_count = x_ref.shape[1] // PTS
    slots, peers = leaves_ref.shape
    wide = GROUP * PTS
    own = iota((GROUP, wide), 1) // PTS == iota((GROUP, wide), 0)
    lane_block = iota((GROUP, LANES), 1) // RANK
    diagonal = iota((columns * GROUP, GROUP * RANK), 1) // RANK == (
        iota((columns * GROUP, GROUP * RANK), 0) % GROUP
    )
    narrow = GROUP * RANK
    tiles = []
    for q in range(leaf_count // GROUP):
        x = x_ref[:, q * wide : (q + 1) * wide]
        spread = jnp.concatenate(
            [jnp.where(own, x[c : c + 1], 0.0) for c in range(columns)], axis=0
        )
        tiles.append(dot3(spread, basis_ref[:, q * wide : (q + 1) * wide], NT))
    lifted = [
        dot3(tile, up_ref[:, q * narrow : (q + 1) * narrow]) for q, tile in enumerate(tiles)
    ]
    skeleton = jnp.concatenate(
        [
            jnp.concatenate(
                [tile[c * GROUP : (c + 1) * GROUP] for c in range(columns)], axis=1
            )
            for tile in tiles
        ],
        axis=0,
    )
    parents = []
    for value in lifted:
        value = fold(jnp.where(diagonal, value, 0.0))
        total = None
        for c in range(columns):
            part = jnp.where(lane_block == c, value[c * GROUP : (c + 1) * GROUP], 0.0)
            total = part if total is None else total + part
        parents.append(jnp.sum(total, axis=0, keepdims=True))
    parents = jnp.concatenate(parents, axis=0)

    wanted = jnp.where(
        iota((slots, peers), 0) < counts_ref[...], leaves_ref[...].astype(F32), -1.0
    )
    rows = peers * slots
    expand = jnp.where(iota((rows, peers), 0) // slots == iota((rows, peers), 1), 1.0, 0.0)
    wanted = mxu(expand.astype(BF16), wanted.astype(BF16), NT)
    wanted = jnp.sum(
        jnp.where(iota((rows, slots), 0) % slots == iota((rows, slots), 1), wanted, 0.0),
        axis=1,
        keepdims=True,
    )
    hot = jnp.where(wanted == iota((rows, leaf_count), 1).astype(F32), 1.0, 0.0).astype(BF16)
    high, low = split(skeleton)
    got = mxu(hot, jnp.concatenate([high, low], axis=1))
    got = got[:, :LANES] + got[:, LANES:]
    send_ref[:, :slots, :] = got.reshape(peers, slots, LANES)
    par_count = parents.shape[0]
    send_ref[:, slots:, :] = jnp.broadcast_to(parents[None], (peers, par_count, LANES))


def pick_kernel(list_in, own_ref, left_ref, right_ref, *rest):
    outs, (table, list_ref, sems) = rest[:-3], rest[-3:]
    copies = fetch((list_in,), (list_ref,), sems)
    columns, points = own_ref.shape
    leaf_count = points // PTS
    groups = len(outs)
    share = list_ref.shape[0] // groups
    base = (lax.axis_index("leaf") - 1) * leaf_count
    me = lax.axis_index("vec")
    for place, ref in enumerate((left_ref, own_ref, right_ref)):
        for b in range(points // LANES):
            tile = ref[:, b * LANES : (b + 1) * LANES]
            tile = jnp.concatenate([tile, tile], axis=0)
            at = place * (points // LANES) + b
            table[0, at] = tile
            table[1, at] = pltpu.roll(tile, PTS, 1)
    lower = iota((2 * columns, LANES), 1) < PTS
    upper_rows = iota((2 * columns, LANES), 0) >= columns
    for copy in copies:
        copy.wait()
    for s, out in enumerate(outs):
        first = lax.rem(me + s, groups) * share
        for pair in range(leaf_count // 2):
            halves = []
            for t in (2 * pair, 2 * pair + 1):
                one = list_ref[first, t] - base
                two = list_ref[first + 1, t] - base
                halves.append(
                    jnp.where(lower, table[one & 1, one >> 1], table[1 - (two & 1), two >> 1])
                )
            out[pair] = jnp.where(upper_rows, halves[1], halves[0])


def near_kernel(blocks_in, *rest):
    blocks_ref, sems = rest[-2:]
    copies = fetch((blocks_in,), (blocks_ref,), sems)
    groups = (len(rest) - 2) // 2
    parts, outs = rest[:groups], rest[groups : 2 * groups]
    columns, points = outs[0].shape
    share = blocks_ref.shape[0]
    lower = iota((columns, LANES), 1) < PTS
    rows = 2 * columns
    per = 2
    for copy in copies:
        copy.wait()
    for g in range(points // (per * LANES)):
        sources = jnp.concatenate(
            [part[g * per + h] for h in range(per) for part in parts], axis=0
        )
        block = blocks_ref[:, :, g * per * LANES : (g + 1) * per * LANES]
        value = dot3(sources, block.reshape(share * PTS, per * LANES))
        for h in range(per):
            for s, out in enumerate(outs):
                at = (h * groups + s) * rows
                tile = value[at : at + rows, h * LANES : (h + 1) * LANES]
                out[:, (g * per + h) * LANES : (g * per + h + 1) * LANES] = jnp.where(
                    lower, tile[:columns], tile[columns:]
                )


def far_kernel(*refs):
    count = 7
    sources, out_ref, targets, (hot_ref, sems) = refs[:7], refs[7], refs[8:15], refs[15:]
    recv_ref, top_ref, slot_ref, top_coupling_ref, down_ref, coupling_ref, basis_ref = targets
    coupling_in = sources[5]
    columns, points = out_ref.shape
    leaf_count = points // PTS
    peers = recv_ref.shape[0]
    par_count = leaf_count // GROUP
    slots = recv_ref.shape[1] - par_count
    far_count = coupling_ref.shape[0]
    top_count = top_coupling_ref.shape[0]
    narrow, wide = GROUP * RANK, GROUP * PTS
    groups = range(par_count)

    def lanes(g, size):
        return slice(g * size, (g + 1) * size)

    copies = []
    for i in range(count):
        if i != 5:
            copies.append(pltpu.make_async_copy(sources[i], targets[i], sems.at[i]))
    copies[5:5] = [
        pltpu.make_async_copy(
            coupling_in.at[:, :, lanes(g, narrow)],
            coupling_ref.at[:, :, lanes(g, narrow)],
            sems.at[count + g],
        )
        for g in groups
    ]
    for copy in copies:
        copy.start()
    rows = columns * GROUP
    diagonal = iota((rows, narrow), 1) // RANK == iota((rows, narrow), 0) % GROUP
    diagonal_out = iota((rows, wide), 1) // PTS == iota((rows, wide), 0) % GROUP

    copies[1].wait()
    copies[2].wait()
    square = iota((leaf_count, leaf_count), 0) == iota((leaf_count, leaf_count), 1)
    square = jnp.where(square, 1.0, 0.0).astype(BF16)
    slot = slot_ref[...]
    slot = mxu(square, (slot >> 5).astype(F32).astype(BF16), NT) * 32.0 + mxu(
        square, (slot & 31).astype(F32).astype(BF16), NT
    )
    hot_top = hot_rows(top_ref[...], peers * par_count)
    hot_ref[...] = hot_rows(slot.astype(jnp.int32), peers * slots)
    copies[0].wait()
    tops = recv_ref[:, slots:, :].reshape(peers * par_count, LANES)
    top_got = pick_rows(hot_top, tops)
    tiles = recv_ref[:, :slots, :].reshape(peers * slots, LANES)
    got = pick_rows(hot_ref[...], tiles)

    for copy in copies[3:5]:
        copy.wait()
    field = dot3(
        by_column([top_got[lanes(j, GROUP)] for j in range(top_count)], columns),
        top_coupling_ref[...].reshape(top_count * RANK, narrow),
    )
    field = fold(jnp.where(diagonal, field, 0.0))[:, :RANK]
    lowered = dot3(field, down_ref[...])

    gathered = [
        by_column(
            [got[lanes(j * par_count + g, GROUP)] for j in range(far_count)],
            columns,
        )
        for g in groups
    ]
    fields = []
    for g in groups:
        copies[5 + g].wait()
        fields.append(
            dot3(
                gathered[g],
                coupling_ref[:, :, lanes(g, narrow)].reshape(far_count * RANK, narrow),
            )
        )
    spread = []
    for g in groups:
        above = jnp.concatenate(
            [
                jnp.broadcast_to(
                    lowered[c * GROUP + g : c * GROUP + g + 1, lanes(g, narrow)], (GROUP, narrow)
                )
                for c in range(columns)
            ],
            axis=0,
        )
        spread.append(fold(jnp.where(diagonal, fields[g] + above, 0.0))[:, :RANK])
    for copy in copies[5 + par_count :]:
        copy.wait()
    values = [dot3(spread[g], basis_ref[:, lanes(g, wide)]) for g in groups]
    for g in groups:
        value = jnp.where(diagonal_out, values[g], 0.0)
        out_ref[:, lanes(g, wide)] = jnp.sum(value.reshape(columns, GROUP, wide), axis=1)


VMEM = pl.BlockSpec(memory_space=pltpu.VMEM)
ANY = pl.BlockSpec(memory_space=pl.ANY)
MIB = 1024 * 1024
UP_MIB, PICK_MIB, NEAR_MIB, FAR_MIB = 60, 24, 24, 60
UP_US, PICK_US, NEAR_US, FAR_US = 2, 2, 8, 4


def cost(micros):
    return pl.CostEstimate(flops=int(micros * 1e9), bytes_accessed=0, transcendentals=0)


def buffers(*arrays):
    return [pltpu.VMEM(array.shape, array.dtype) for array in arrays] + [
        pltpu.SemaphoreType.DMA((len(arrays),))
    ]


def local(
    points_x,
    near_list,
    near_blocks,
    leaf_basis,
    out_basis,
    up_transfer,
    down_transfer,
    send_leaves,
    send_counts,
    recv_slot,
    leaf_coupling,
    top_list,
    top_coupling,
):
    columns, points = points_x.shape
    leaf_count = near_list.shape[0]
    par_count = top_list.shape[0]
    peers, slots = send_leaves.shape[1:]
    groups = lax.axis_size("vec")
    ring = lax.axis_size("leaf")

    left = lax.ppermute(points_x, "leaf", [(i, (i + 1) % ring) for i in range(ring)])
    right = lax.ppermute(points_x, "leaf", [((i + 1) % ring, i) for i in range(ring)])

    up_args = (points_x, leaf_basis, up_transfer, send_leaves[0].T, send_counts)
    send = pl.pallas_call(
        up_kernel,
        name="up",
        out_shape=jax.ShapeDtypeStruct((peers, slots + par_count, LANES), F32),
        in_specs=[ANY] * 5,
        out_specs=VMEM,
        scratch_shapes=buffers(*up_args),
        compiler_params=pltpu.CompilerParams(vmem_limit_bytes=UP_MIB * MIB),
        cost_estimate=cost(UP_US),
    )(*up_args)
    recv = lax.all_to_all(send, "leaf", split_axis=0, concat_axis=0, tiled=True)

    picked = pl.pallas_call(
        pick_kernel,
        name="pick",
        out_shape=[jax.ShapeDtypeStruct((leaf_count // 2, 2 * columns, LANES), F32)] * groups,
        in_specs=[ANY] + [VMEM] * 3,
        out_specs=[VMEM] * groups,
        scratch_shapes=[
            pltpu.VMEM((2, 3 * points // LANES, 2 * columns, LANES), F32),
            pltpu.SMEM(near_list.T.shape, jnp.int32),
            pltpu.SemaphoreType.DMA((1,)),
        ],
        compiler_params=pltpu.CompilerParams(vmem_limit_bytes=PICK_MIB * MIB),
        cost_estimate=cost(PICK_US),
    )(near_list.T, points_x, left, right)
    parts = [picked[0]] + [
        lax.ppermute(picked[s], "vec", [(i, (i + s) % groups) for i in range(groups)])
        for s in range(1, groups)
    ]

    partial = pl.pallas_call(
        near_kernel,
        name="near",
        out_shape=[jax.ShapeDtypeStruct((columns, points), F32)] * groups,
        in_specs=[ANY] + [VMEM] * groups,
        out_specs=[VMEM] * groups,
        scratch_shapes=buffers(near_blocks),
        compiler_params=pltpu.CompilerParams(vmem_limit_bytes=NEAR_MIB * MIB),
        cost_estimate=cost(NEAR_US),
    )(near_blocks, *parts)
    sums = [partial[0]] + [
        lax.ppermute(partial[s], "vec", [(i, (i - s) % groups) for i in range(groups)])
        for s in range(1, groups)
    ]
    far_args = [
        recv,
        top_list,
        recv_slot.T,
        top_coupling,
        down_transfer,
        leaf_coupling,
        out_basis,
    ]
    far = pl.pallas_call(
        far_kernel,
        name="far",
        out_shape=jax.ShapeDtypeStruct((columns, points), F32),
        in_specs=[ANY] * len(far_args),
        out_specs=VMEM,
        scratch_shapes=[pltpu.VMEM(array.shape, array.dtype) for array in far_args]
        + [
            pltpu.VMEM((recv_slot.size, peers * slots), BF16),
            pltpu.SemaphoreType.DMA((len(far_args) + par_count,)),
        ],
        compiler_params=pltpu.CompilerParams(vmem_limit_bytes=FAR_MIB * MIB),
        cost_estimate=cost(FAR_US),
    )(*far_args)
    return far + sum(sums[1:], sums[0])


def solution(mesh):
    placed = (
        P("vec", "leaf"),
        P("leaf", None),
        P("vec", None, "leaf"),
        P(None, "leaf"),
        P(None, "leaf"),
        P(None, "leaf"),
        P(None, "leaf"),
        P("leaf", None, None),
        P("leaf", None),
        P("leaf", None),
        P(None, None, "leaf"),
        P("leaf", None),
        P(None, None, "leaf"),
    )
    return jax.shard_map(
        local, mesh=mesh, in_specs=placed, out_specs=P("vec", "leaf"), check_vma=False
    )
```

time: 57.2 us -> 45.5 us (0.80)
  the two profiles are of different devices: /device:TPU:2 before, /device:TPU:8 now
where the time goes in v2:
time: 45.5 us; the launch traced here: 45.3 us
  starting transfers between devices  26.3 us (58%)
  Pallas kernels  11.7 us (26%)
  waiting for transfers between devices  4.91 us (11%)
  other arithmetic  1.51 us (3%)
  local copies, waits for them, and re-layouts  0.8 us (2%)
    all_to_all x1, starting transfers between devices, local(): recv = lax.all_to_all(send, 'leaf', split_axis=0, concat_axis=0, tiled=True)  10 us
    pallas_call x1, Pallas kernels, local(): pl.pallas_call(far_kernel, name='far', out_shape=jax.ShapeDtypeStruct((co...  6.2 us
    ppermute x3, starting transfers between devices, local(): lax.ppermute(picked[s], 'vec', [(i, (i + s) % groups) for i in range(grou...  5.74 us
    ppermute x3, starting transfers between devices, local(): lax.ppermute(partial[s], 'vec', [(i, (i - s) % groups) for i in range(gro...  5.37 us
    ppermute x1, starting transfers between devices, local(): lax.ppermute(points_x, 'leaf', [((i + 1) % ring, i) for i in range(ring)])  5.18 us
    ppermute x3, waiting for transfers between devices, local(): lax.ppermute(picked[s], 'vec', [(i, (i + s) % groups) for i in range(grou...  4.9 us
    pallas_call x1, Pallas kernels, local(): pl.pallas_call(up_kernel, name='up', out_shape=jax.ShapeDtypeStruct((peer...  2.82 us
    pallas_call x1, Pallas kernels, local(): pl.pallas_call(pick_kernel, name='pick', out_shape=[jax.ShapeDtypeStruct(...  1.91 us
  transfers between devices with their start and end apart: 9, of which 2 were waited for; matrix products, arithmetic and copies ran while one was open for 0% of the time, Pallas kernels for 26%

profile of v2, /device:TPU:8, one launch (start us, length us, event | category | flops | bytes accessed | tf_op | source)
XLA Modules:
  0.0 45.3 jit_solution(11645854767834686364)
XLA Ops:
  0.0 0.0 collective-permute-start
  0.0 5.2 %collective-permute-start.1 = (f32[4,4096]{1,0:T(4,128)}, f32[4,4096]{1,0:T(4,128)S(1)}, u32[]{:S(2)}, u32[]{:S(2)}) collective-permute-start(f32[4,4096]{1,0:T(4,128)} %own_ref.1), channel_id=1, source_target_pairs={{4,0},{8,4},{12,8},{16,12},{20,16},{24,20},{28,24},{32,28},{36,32}... | collective-permute-start | bytes 196616 | tf_op jit(solution)/shard_map/ppermute | solution.py:352
  5.2 0.0 copy-start.1
  5.2 0.0 copy-start.2
  5.2 2.8 %up.1 = f32[64,16,128]{2,1,0:T(8,128)} custom-call(f32[4,4096]{1,0:T(4,128)} %own_ref.1, f32[32,4096]{1,0:T(8,128)} %basis_in.1, f32[32,2048]{1,0:T(8,128)} %up_in.1, s32[8,64]{1,0:T(8,128)} %bitcast.7, s32[1,64]{1,0:T(1,128)} %counts_in.1), custom_call_target="tpu_custom_call" | custom-call | flops 2000000000 | tf_op jit(solution)/shard_map/up/pallas_call | solution.py:355
  8.0 0.0 copy-start
  8.0 10.0 %all-to-all-start = ((f32[64,16,128]{2,1,0:T(8,128)}), f32[64,16,128]{2,1,0:T(8,128)S(1)}, u32[]{:S(2)}, u32[]{:S(2)}) async-start(f32[64,16,128]{2,1,0:T(8,128)} %up.1), calls=%async_computation | async-start | bytes 1048576 | tf_op jit(solution)/shard_map/all_to_all | solution.py:365
  18.1 0.0 collective-permute-done.left_ref
  18.1 0.0 collective-permute-done.1.right_ref
  18.1 0.0 copy-done.1
  18.1 0.0 copy-done.2
  18.1 1.9 %pick.1 = (f32[32,8,128]{2,1,0:T(8,128)S(1)}, f32[32,8,128]{2,1,0:T(8,128)S(1)}, f32[32,8,128]{2,1,0:T(8,128)S(1)}, f32[32,8,128]{2,1,0:T(8,128)S(1)}) custom-call(s32[8,64]{1,0:T(8,128)S(1)} %bitcast.5, f32[4,4096]{1,0:T(4,128)S(1)} %copy-done.1, f32[4,4096]{1,0:T(4,128)S(1)} %collective-permute-done.left_ref, f32[4,4096]{1,0:T(4,128)S(1)} %collective-permute-done.1.right_ref), custom_call_target="tpu_custom_call" | custom-call | flops 2000000000 | tf_op jit(solution)/shard_map/pick/pallas_call | solution.py:367
  20.0 1.6 %collective-permute-start.2 = (f32[32,8,128]{2,1,0:T(8,128)S(1)}, f32[32,8,128]{2,1,0:T(8,128)S(1)}, u32[]{:S(2)}, u32[]{:S(2)}) collective-permute-start(f32[32,8,128]{2,1,0:T(8,128)S(1)} %get-tuple-element.14), channel_id=1, source_target_pairs={{0,1},{1,2},{2,3},{3,0},{4,5},{5,6},{6,7},{7,4},{8,9},{9,10},{10,1... | collective-permute-start | bytes 393224 | tf_op jit(solution)/shard_map/ppermute | solution.py:382
  21.6 2.7 %collective-permute-start.3 = (f32[32,8,128]{2,1,0:T(8,128)S(1)}, f32[32,8,128]{2,1,0:T(8,128)S(1)}, u32[]{:S(2)}, u32[]{:S(2)}) collective-permute-start(f32[32,8,128]{2,1,0:T(8,128)S(1)} %get-tuple-element.15), channel_id=1, source_target_pairs={{0,2},{1,3},{2,0},{3,1},{4,6},{5,7},{6,4},{7,5},{8,10},{9,11},{10,... | collective-permute-start | bytes 393224 | tf_op jit(solution)/shard_map/ppermute | solution.py:382
  24.3 1.4 %collective-permute-start.4 = (f32[32,8,128]{2,1,0:T(8,128)S(1)}, f32[32,8,128]{2,1,0:T(8,128)S(1)}, u32[]{:S(2)}, u32[]{:S(2)}) collective-permute-start(f32[32,8,128]{2,1,0:T(8,128)S(1)} %get-tuple-element.16), channel_id=1, source_target_pairs={{0,3},{1,0},{2,1},{3,2},{4,7},{5,4},{6,5},{7,6},{8,11},{9,8},{10,9... | collective-permute-start | bytes 393224 | tf_op jit(solution)/shard_map/ppermute | solution.py:382
  25.8 1.1 %collective-permute-done.2.rest_1_ = f32[32,8,128]{2,1,0:T(8,128)S(1)} collective-permute-done((f32[32,8,128]{2,1,0:T(8,128)S(1)}, f32[32,8,128]{2,1,0:T(8,128)S(1)}, u32[]{:S(2)}, u32[]{:S(2)}) %collective-permute-start.2) | collective-permute-done | bytes 131104 | tf_op jit(solution)/shard_map/ppermute | solution.py:382
  26.9 3.8 %collective-permute-done.3.rest_2_ = f32[32,8,128]{2,1,0:T(8,128)S(1)} collective-permute-done((f32[32,8,128]{2,1,0:T(8,128)S(1)}, f32[32,8,128]{2,1,0:T(8,128)S(1)}, u32[]{:S(2)}, u32[]{:S(2)}) %collective-permute-start.3) | collective-permute-done | bytes 131104 | tf_op jit(solution)/shard_map/ppermute | solution.py:382
  30.7 0.0 collective-permute-done.4.rest_3_
  30.7 0.0 copy-done
  30.7 0.7 %near.1 = (f32[4,4096]{1,0:T(4,128)S(1)}, f32[4,4096]{1,0:T(4,128)S(1)}, f32[4,4096]{1,0:T(4,128)S(1)}, f32[4,4096]{1,0:T(4,128)S(1)}) custom-call(f32[2,64,4096]{2,1,0:T(8,128)S(1)} %copy-done, f32[32,8,128]{2,1,0:T(8,128)S(1)} %get-tuple-element.13.rest_0_, f32[32,8,128]{2,1,0:T(8,128)S(1)} %collective-permute-done.2.rest_1_, ...), custom_call_target="tpu_custom_call" | custom-call | flops 8000000000 | tf_op jit(solution)/shard_map/near/pallas_call | solution.py:386
  31.4 1.4 %collective-permute-start.7 = (f32[4,4096]{1,0:T(4,128)S(1)}, f32[4,4096]{1,0:T(4,128)S(1)}, u32[]{:S(2)}, u32[]{:S(2)}) collective-permute-start(f32[4,4096]{1,0:T(4,128)S(1)} %get-tuple-element.20), channel_id=1, source_target_pairs={{0,1},{1,2},{2,3},{3,0},{4,5},{5,6},{6,7},{7,4},{8,9},{9,10},{10,1... | collective-permute-start | bytes 196616 | tf_op jit(solution)/shard_map/ppermute | solution.py:397
  32.8 2.4 %collective-permute-start.6 = (f32[4,4096]{1,0:T(4,128)S(1)}, f32[4,4096]{1,0:T(4,128)S(1)}, u32[]{:S(2)}, u32[]{:S(2)}) collective-permute-start(f32[4,4096]{1,0:T(4,128)S(1)} %get-tuple-element.19), channel_id=1, source_target_pairs={{0,2},{1,3},{2,0},{3,1},{4,6},{5,7},{6,4},{7,5},{8,10},{9,11},{10,... | collective-permute-start | bytes 196616 | tf_op jit(solution)/shard_map/ppermute | solution.py:397
  35.2 1.6 %collective-permute-start.5 = (f32[4,4096]{1,0:T(4,128)S(1)}, f32[4,4096]{1,0:T(4,128)S(1)}, u32[]{:S(2)}, u32[]{:S(2)}) collective-permute-start(f32[4,4096]{1,0:T(4,128)S(1)} %get-tuple-element.18), channel_id=1, source_target_pairs={{0,3},{1,0},{2,1},{3,2},{4,7},{5,4},{6,5},{7,6},{8,11},{9,8},{10,9... | collective-permute-start | bytes 196616 | tf_op jit(solution)/shard_map/ppermute | solution.py:397
  36.8 0.0 all-to-all-done.refs_0_
  36.8 0.0 copy-start.3
  36.8 0.8 %copy-done.3 = f32[64,16,128]{2,1,0:T(8,128)} copy-done((f32[64,16,128]{2,1,0:T(8,128)}, f32[64,16,128]{2,1,0:T(8,128)S(1)}, u32[]{:S(2)}) %copy-start.3) | copy-done | bytes 524312
  37.6 6.2 %far.1 = f32[4,4096]{1,0:T(4,128)} custom-call(f32[64,16,128]{2,1,0:T(8,128)} %copy-done.3, s32[8,8]{1,0:T(8,128)} %refs_1_.1, s32[16,64]{1,0:T(8,128)} %bitcast.6, f32[8,32,256]{2,1,0:T(8,128)} %refs_3_.1, f32[32,2048]{1,0:T(8,128)} %refs_4_.1, f32[16,32,2048]{2,1,0:T(8,128)} %refs_5_.1, f32[32,4096]{1,0:T(8,128)} %refs_6_.1), custom_call_target="tpu_custom_call" | custom-call | flops 4000000000 | tf_op jit(solution)/shard_map/far/pallas_call | solution.py:409
  43.8 0.0 collective-permute-done.7
  43.8 0.0 collective-permute-done.6
  43.8 0.0 collective-permute-done.5
  43.8 1.5 %add_add_fusion = f32[4,4096]{1,0:T(4,128)} fusion(f32[4,4096]{1,0:T(4,128)} %far.1, f32[4,4096]{1,0:T(4,128)S(1)} %collective-permute-done.7, f32[4,4096]{1,0:T(4,128)S(1)} %collective-permute-done.6, f32[4,4096]{1,0:T(4,128)S(1)} %get-tuple-element.17, f32[4,4096]{1,0:T(4,128)S(1)} %collective-permute-done.5), kind=kLoop, calls=%fused_computation | loop fusion | flops 65536 | bytes 393216 | tf_op jit(solution)/shard_map/add | solution.py:423
Async XLA Ops:
  0.0 18.1 %collective-permute-start = (f32[4,4096]{1,0:T(4,128)}, f32[4,4096]{1,0:T(4,128)S(1)}, u32[]{:S(2)}, u32[]{:S(2)}) collective-permute-start(f32[4,4096]{1,0:T(4,128)} %own_ref.1), channel_id=1, source_target_pairs={{0,4},{4,8},{8,12},{12,16},{16,20},{20,24},{24,28},{28,32},{32,36}... | collective-permute-start | bytes 196616 | tf_op jit(solution)/shard_map/ppermute | solution.py:351
  0.0 18.1 %collective-permute-start.1 = (f32[4,4096]{1,0:T(4,128)}, f32[4,4096]{1,0:T(4,128)S(1)}, u32[]{:S(2)}, u32[]{:S(2)}) collective-permute-start(f32[4,4096]{1,0:T(4,128)} %own_ref.1), channel_id=1, source_target_pairs={{4,0},{8,4},{12,8},{16,12},{20,16},{24,20},{28,24},{32,28},{36,32}... | collective-permute-start | bytes 196616 | tf_op jit(solution)/shard_map/ppermute | solution.py:352
  5.2 12.9 %copy-start.1 = (f32[4,4096]{1,0:T(4,128)S(1)}, f32[4,4096]{1,0:T(4,128)}, u32[]{:S(2)}) copy-start(f32[4,4096]{1,0:T(4,128)} %own_ref.1) | copy-start | bytes 196612
  5.2 12.9 %copy-start.2 = (s32[64,8]{0,1:T(8,128)S(1)}, s32[64,8]{0,1:T(8,128)}, u32[]{:S(2)}) copy-start(s32[64,8]{0,1:T(8,128)} %param.14) | copy-start | bytes 6148
  8.0 22.6 %copy-start = (f32[2,64,4096]{2,1,0:T(8,128)S(1)}, f32[2,64,4096]{2,1,0:T(8,128)}, u32[]{:S(2)}) copy-start(f32[2,64,4096]{2,1,0:T(8,128)} %blocks_in.1) | copy-start | bytes 6291460
  8.0 28.7 %all-to-all-start = ((f32[64,16,128]{2,1,0:T(8,128)}), f32[64,16,128]{2,1,0:T(8,128)S(1)}, u32[]{:S(2)}, u32[]{:S(2)}) async-start(f32[64,16,128]{2,1,0:T(8,128)} %up.1), calls=%async_computation | async-start | bytes 1048576 | tf_op jit(solution)/shard_map/all_to_all | solution.py:365
  20.0 6.8 %collective-permute-start.2 = (f32[32,8,128]{2,1,0:T(8,128)S(1)}, f32[32,8,128]{2,1,0:T(8,128)S(1)}, u32[]{:S(2)}, u32[]{:S(2)}) collective-permute-start(f32[32,8,128]{2,1,0:T(8,128)S(1)} %get-tuple-element.14), channel_id=1, source_target_pairs={{0,1},{1,2},{2,3},{3,0},{4,5},{5,6},{6,7},{7,4},{8,9},{9,10},{10,1... | collective-permute-start | bytes 393224 | tf_op jit(solution)/shard_map/ppermute | solution.py:382
  21.6 9.1 %collective-permute-start.3 = (f32[32,8,128]{2,1,0:T(8,128)S(1)}, f32[32,8,128]{2,1,0:T(8,128)S(1)}, u32[]{:S(2)}, u32[]{:S(2)}) collective-permute-start(f32[32,8,128]{2,1,0:T(8,128)S(1)} %get-tuple-element.15), channel_id=1, source_target_pairs={{0,2},{1,3},{2,0},{3,1},{4,6},{5,7},{6,4},{7,5},{8,10},{9,11},{10,... | collective-permute-start | bytes 393224 | tf_op jit(solution)/shard_map/ppermute | solution.py:382
  24.3 6.3 %collective-permute-start.4 = (f32[32,8,128]{2,1,0:T(8,128)S(1)}, f32[32,8,128]{2,1,0:T(8,128)S(1)}, u32[]{:S(2)}, u32[]{:S(2)}) collective-permute-start(f32[32,8,128]{2,1,0:T(8,128)S(1)} %get-tuple-element.16), channel_id=1, source_target_pairs={{0,3},{1,0},{2,1},{3,2},{4,7},{5,4},{6,5},{7,6},{8,11},{9,8},{10,9... | collective-permute-start | bytes 393224 | tf_op jit(solution)/shard_map/ppermute | solution.py:382
  31.4 12.4 %collective-permute-start.7 = (f32[4,4096]{1,0:T(4,128)S(1)}, f32[4,4096]{1,0:T(4,128)S(1)}, u32[]{:S(2)}, u32[]{:S(2)}) collective-permute-start(f32[4,4096]{1,0:T(4,128)S(1)} %get-tuple-element.20), channel_id=1, source_target_pairs={{0,1},{1,2},{2,3},{3,0},{4,5},{5,6},{6,7},{7,4},{8,9},{9,10},{10,1... | collective-permute-start | bytes 196616 | tf_op jit(solution)/shard_map/ppermute | solution.py:397
  32.8 11.0 %collective-permute-start.6 = (f32[4,4096]{1,0:T(4,128)S(1)}, f32[4,4096]{1,0:T(4,128)S(1)}, u32[]{:S(2)}, u32[]{:S(2)}) collective-permute-start(f32[4,4096]{1,0:T(4,128)S(1)} %get-tuple-element.19), channel_id=1, source_target_pairs={{0,2},{1,3},{2,0},{3,1},{4,6},{5,7},{6,4},{7,5},{8,10},{9,11},{10,... | collective-permute-start | bytes 196616 | tf_op jit(solution)/shard_map/ppermute | solution.py:397
  35.2 8.6 %collective-permute-start.5 = (f32[4,4096]{1,0:T(4,128)S(1)}, f32[4,4096]{1,0:T(4,128)S(1)}, u32[]{:S(2)}, u32[]{:S(2)}) collective-permute-start(f32[4,4096]{1,0:T(4,128)S(1)} %get-tuple-element.18), channel_id=1, source_target_pairs={{0,3},{1,0},{2,1},{3,2},{4,7},{5,4},{6,5},{7,6},{8,11},{9,8},{10,9... | collective-permute-start | bytes 196616 | tf_op jit(solution)/shard_map/ppermute | solution.py:397
  36.8 0.8 %copy-start.3 = (f32[64,16,128]{2,1,0:T(8,128)}, f32[64,16,128]{2,1,0:T(8,128)S(1)}, u32[]{:S(2)}) copy-start(f32[64,16,128]{2,1,0:T(8,128)S(1)} %all-to-all-done.refs_0_) | copy-start | bytes 1572868

commit v3 on v2

--- a/solution.py
+++ b/solution.py
@@ -213,10 +213,15 @@
 
 
 def far_kernel(*refs):
-    count = 7
-    sources, out_ref, targets, (hot_ref, sems) = refs[:7], refs[7], refs[8:15], refs[15:]
-    recv_ref, top_ref, slot_ref, top_coupling_ref, down_ref, coupling_ref, basis_ref = targets
-    coupling_in = sources[5]
+    recv_ref, sources, out_ref, targets, (hot_ref, sems) = (
+        refs[0],
+        refs[1:7],
+        refs[7],
+        refs[8:14],
+        refs[14:],
+    )
+    top_ref, slot_ref, top_coupling_ref, down_ref, coupling_ref, basis_ref = targets
+    coupling_in = sources[4]
     columns, points = out_ref.shape
     leaf_count = points // PTS
     peers = recv_ref.shape[0]
@@ -230,15 +235,14 @@
     def lanes(g, size):
         return slice(g * size, (g + 1) * size)
 
-    copies = []
-    for i in range(count):
-        if i != 5:
-            copies.append(pltpu.make_async_copy(sources[i], targets[i], sems.at[i]))
-    copies[5:5] = [
+    copies = [
+        pltpu.make_async_copy(sources[i], targets[i], sems.at[i]) for i in (0, 1, 2, 3, 5)
+    ]
+    copies[4:4] = [
         pltpu.make_async_copy(
             coupling_in.at[:, :, lanes(g, narrow)],
             coupling_ref.at[:, :, lanes(g, narrow)],
-            sems.at[count + g],
+            sems.at[6 + g],
         )
         for g in groups
     ]
@@ -248,8 +252,8 @@
     diagonal = iota((rows, narrow), 1) // RANK == iota((rows, narrow), 0) % GROUP
     diagonal_out = iota((rows, wide), 1) // PTS == iota((rows, wide), 0) % GROUP
 
+    copies[0].wait()
     copies[1].wait()
-    copies[2].wait()
     square = iota((leaf_count, leaf_count), 0) == iota((leaf_count, leaf_count), 1)
     square = jnp.where(square, 1.0, 0.0).astype(BF16)
     slot = slot_ref[...]
@@ -258,13 +262,12 @@
     )
     hot_top = hot_rows(top_ref[...], peers * par_count)
     hot_ref[...] = hot_rows(slot.astype(jnp.int32), peers * slots)
-    copies[0].wait()
     tops = recv_ref[:, slots:, :].reshape(peers * par_count, LANES)
     top_got = pick_rows(hot_top, tops)
     tiles = recv_ref[:, :slots, :].reshape(peers * slots, LANES)
     got = pick_rows(hot_ref[...], tiles)
 
-    for copy in copies[3:5]:
+    for copy in copies[2:4]:
         copy.wait()
     field = dot3(
         by_column([top_got[lanes(j, GROUP)] for j in range(top_count)], columns),
@@ -282,7 +285,7 @@
     ]
     fields = []
     for g in groups:
-        copies[5 + g].wait()
+        copies[4 + g].wait()
         fields.append(
             dot3(
                 gathered[g],
@@ -301,7 +304,7 @@
             axis=0,
         )
         spread.append(fold(jnp.where(diagonal, fields[g] + above, 0.0))[:, :RANK])
-    for copy in copies[5 + par_count :]:
+    for copy in copies[4 + par_count :]:
         copy.wait()
     values = [dot3(spread[g], basis_ref[:, lanes(g, wide)]) for g in groups]
     for g in groups:
@@ -312,7 +315,7 @@
 VMEM = pl.BlockSpec(memory_space=pltpu.VMEM)
 ANY = pl.BlockSpec(memory_space=pl.ANY)
 MIB = 1024 * 1024
-UP_MIB, PICK_MIB, NEAR_MIB, FAR_MIB = 60, 24, 24, 60
+UP_MIB, PICK_MIB, NEAR_MIB, FAR_MIB = 60, 24, 24, 51
 UP_US, PICK_US, NEAR_US, FAR_US = 2, 2, 8, 4
 
 
@@ -398,7 +401,6 @@
         for s in range(1, groups)
     ]
     far_args = [
-        recv,
         top_list,
         recv_slot.T,
         top_coupling,
@@ -410,7 +412,7 @@
         far_kernel,
         name="far",
         out_shape=jax.ShapeDtypeStruct((columns, points), F32),
-        in_specs=[ANY] * len(far_args),
+        in_specs=[VMEM] + [ANY] * len(far_args),
         out_specs=VMEM,
         scratch_shapes=[pltpu.VMEM(array.shape, array.dtype) for array in far_args]
         + [
@@ -419,7 +421,7 @@
         ],
         compiler_params=pltpu.CompilerParams(vmem_limit_bytes=FAR_MIB * MIB),
         cost_estimate=cost(FAR_US),
-    )(*far_args)
+    )(recv, *far_args)
     return far + sum(sums[1:], sums[0])
 
 

time: 45.5 us -> 43.8 us (0.963)
  Pallas kernels: 11.7 us -> 10.6 us
  other arithmetic: 1.51 us -> 0.67 us
    pallas_call x1, Pallas kernels: 6.2 us -> 4.48 us  [local(): pl.pallas_call(far_kernel, name='far', out_shape=jax.ShapeDtypeStruct((co...]
    add x1, other arithmetic: 1.51 us -> 0.67 us  [local(): return far + sum(sums[1:], sums[0])]
    pallas_call x1, Pallas kernels: 0.72 us -> 1.36 us  [local(): pl.pallas_call(near_kernel, name='near', out_shape=[jax.ShapeDtypeStruct(...]
    unnamed x8 -> x16, local copies, waits for them, and re-layouts: 0.8 us -> 0.98 us
  transfers between devices with their start and end apart: 9 -> 9, of which waited for: 2 -> 2; matrix products, arithmetic and copies ran while one was open for 0% -> 0% of each run, Pallas kernels for 26% -> 24%
where the time goes in v3:
time: 43.8 us; the launch traced here: 43.6 us
  starting transfers between devices  26.3 us (60%)
  Pallas kernels  10.6 us (24%)
  waiting for transfers between devices  4.91 us (11%)
  local copies, waits for them, and re-layouts  0.98 us (2%)
  other arithmetic  0.67 us (2%)
    all_to_all x1, starting transfers between devices, local(): recv = lax.all_to_all(send, 'leaf', split_axis=0, concat_axis=0, tiled=True)  10 us
    ppermute x3, starting transfers between devices, local(): lax.ppermute(picked[s], 'vec', [(i, (i + s) % groups) for i in range(grou...  5.74 us
    ppermute x3, starting transfers between devices, local(): lax.ppermute(partial[s], 'vec', [(i, (i - s) % groups) for i in range(gro...  5.36 us
    ppermute x1, starting transfers between devices, local(): lax.ppermute(points_x, 'leaf', [((i + 1) % ring, i) for i in range(ring)])  5.18 us
    ppermute x3, waiting for transfers between devices, local(): lax.ppermute(picked[s], 'vec', [(i, (i + s) % groups) for i in range(grou...  4.9 us
    pallas_call x1, Pallas kernels, local(): pl.pallas_call(far_kernel, name='far', out_shape=jax.ShapeDtypeStruct((co...  4.48 us
    pallas_call x1, Pallas kernels, local(): pl.pallas_call(up_kernel, name='up', out_shape=jax.ShapeDtypeStruct((peer...  2.83 us
    pallas_call x1, Pallas kernels, local(): pl.pallas_call(pick_kernel, name='pick', out_shape=[jax.ShapeDtypeStruct(...  1.91 us
  transfers between devices with their start and end apart: 9, of which 2 were waited for; matrix products, arithmetic and copies ran while one was open for 0% of the time, Pallas kernels for 24%

profile of v3, /device:TPU:8, one launch (start us, length us, event | category | flops | bytes accessed | tf_op | source)
XLA Modules:
  0.0 43.6 jit_solution(3201057634480812905)
XLA Ops:
  0.0 0.0 collective-permute-start
  0.0 5.2 %collective-permute-start.1 = (f32[4,4096]{1,0:T(4,128)}, f32[4,4096]{1,0:T(4,128)S(1)}, u32[]{:S(2)}, u32[]{:S(2)}) collective-permute-start(f32[4,4096]{1,0:T(4,128)} %own_ref.1), channel_id=1, source_target_pairs={{4,0},{8,4},{12,8},{16,12},{20,16},{24,20},{28,24},{32,28},{36,32}... | collective-permute-start | bytes 196616 | tf_op jit(solution)/shard_map/ppermute | solution.py:355
  5.2 0.0 copy-start.4
  5.2 0.0 copy-start.6
  5.2 2.8 %up.1 = f32[64,16,128]{2,1,0:T(8,128)} custom-call(f32[4,4096]{1,0:T(4,128)} %own_ref.1, f32[32,4096]{1,0:T(8,128)} %basis_in.1, f32[32,2048]{1,0:T(8,128)} %up_in.1, s32[8,64]{1,0:T(8,128)} %bitcast.7, s32[1,64]{1,0:T(1,128)} %counts_in.1), custom_call_target="tpu_custom_call" | custom-call | flops 2000000000 | tf_op jit(solution)/shard_map/up/pallas_call | solution.py:358
  8.0 0.0 copy-start
  8.0 10.0 %all-to-all-start = ((f32[64,16,128]{2,1,0:T(8,128)}), f32[64,16,128]{2,1,0:T(8,128)S(1)}, u32[]{:S(2)}, u32[]{:S(2)}) async-start(f32[64,16,128]{2,1,0:T(8,128)} %up.1), calls=%async_computation | async-start | bytes 1048576 | tf_op jit(solution)/shard_map/all_to_all | solution.py:368
  18.1 0.0 collective-permute-done.left_ref
  18.1 0.0 collective-permute-done.1.right_ref
  18.1 0.0 copy-done.4
  18.1 0.0 copy-done.6
  18.1 1.9 %pick.1 = (f32[32,8,128]{2,1,0:T(8,128)S(1)}, f32[32,8,128]{2,1,0:T(8,128)S(1)}, f32[32,8,128]{2,1,0:T(8,128)S(1)}, f32[32,8,128]{2,1,0:T(8,128)S(1)}) custom-call(s32[8,64]{1,0:T(8,128)S(1)} %bitcast.6, f32[4,4096]{1,0:T(4,128)S(1)} %copy-done.4, f32[4,4096]{1,0:T(4,128)S(1)} %collective-permute-done.left_ref, f32[4,4096]{1,0:T(4,128)S(1)} %collective-permute-done.1.right_ref), custom_call_target="tpu_custom_call" | custom-call | flops 2000000000 | tf_op jit(solution)/shard_map/pick/pallas_call | solution.py:370
  20.0 1.6 %collective-permute-start.2 = (f32[32,8,128]{2,1,0:T(8,128)S(1)}, f32[32,8,128]{2,1,0:T(8,128)S(1)}, u32[]{:S(2)}, u32[]{:S(2)}) collective-permute-start(f32[32,8,128]{2,1,0:T(8,128)S(1)} %get-tuple-element.14), channel_id=1, source_target_pairs={{0,1},{1,2},{2,3},{3,0},{4,5},{5,6},{6,7},{7,4},{8,9},{9,10},{10,1... | collective-permute-start | bytes 393224 | tf_op jit(solution)/shard_map/ppermute | solution.py:385
  21.6 2.7 %collective-permute-start.3 = (f32[32,8,128]{2,1,0:T(8,128)S(1)}, f32[32,8,128]{2,1,0:T(8,128)S(1)}, u32[]{:S(2)}, u32[]{:S(2)}) collective-permute-start(f32[32,8,128]{2,1,0:T(8,128)S(1)} %get-tuple-element.15), channel_id=1, source_target_pairs={{0,2},{1,3},{2,0},{3,1},{4,6},{5,7},{6,4},{7,5},{8,10},{9,11},{10,... | collective-permute-start | bytes 393224 | tf_op jit(solution)/shard_map/ppermute | solution.py:385
  24.3 1.4 %collective-permute-start.4 = (f32[32,8,128]{2,1,0:T(8,128)S(1)}, f32[32,8,128]{2,1,0:T(8,128)S(1)}, u32[]{:S(2)}, u32[]{:S(2)}) collective-permute-start(f32[32,8,128]{2,1,0:T(8,128)S(1)} %get-tuple-element.16), channel_id=1, source_target_pairs={{0,3},{1,0},{2,1},{3,2},{4,7},{5,4},{6,5},{7,6},{8,11},{9,8},{10,9... | collective-permute-start | bytes 393224 | tf_op jit(solution)/shard_map/ppermute | solution.py:385
  25.8 1.1 %collective-permute-done.2.rest_1_ = f32[32,8,128]{2,1,0:T(8,128)S(1)} collective-permute-done((f32[32,8,128]{2,1,0:T(8,128)S(1)}, f32[32,8,128]{2,1,0:T(8,128)S(1)}, u32[]{:S(2)}, u32[]{:S(2)}) %collective-permute-start.2) | collective-permute-done | bytes 131104 | tf_op jit(solution)/shard_map/ppermute | solution.py:385
  26.9 3.8 %collective-permute-done.3.rest_2_ = f32[32,8,128]{2,1,0:T(8,128)S(1)} collective-permute-done((f32[32,8,128]{2,1,0:T(8,128)S(1)}, f32[32,8,128]{2,1,0:T(8,128)S(1)}, u32[]{:S(2)}, u32[]{:S(2)}) %collective-permute-start.3) | collective-permute-done | bytes 131104 | tf_op jit(solution)/shard_map/ppermute | solution.py:385
  30.7 0.0 collective-permute-done.4.rest_3_
  30.7 0.0 copy-done
  30.7 0.0 copy-start.1
  30.7 0.0 copy-start.2
  30.7 0.0 copy-start.5
  30.7 0.0 copy-start.7
  30.7 1.4 %near.1 = (f32[4,4096]{1,0:T(4,128)S(1)}, f32[4,4096]{1,0:T(4,128)S(1)}, f32[4,4096]{1,0:T(4,128)}, f32[4,4096]{1,0:T(4,128)}) custom-call(f32[2,64,4096]{2,1,0:T(8,128)S(1)} %copy-done, f32[32,8,128]{2,1,0:T(8,128)S(1)} %get-tuple-element.13.rest_0_, f32[32,8,128]{2,1,0:T(8,128)S(1)} %collective-permute-done.2.rest_1_, ...), custom_call_target="tpu_custom_call" | custom-call | flops 8000000000 | tf_op jit(solution)/shard_map/near/pallas_call | solution.py:389
  32.1 1.4 %collective-permute-start.7 = (f32[4,4096]{1,0:T(4,128)}, f32[4,4096]{1,0:T(4,128)S(1)}, u32[]{:S(2)}, u32[]{:S(2)}) collective-permute-start(f32[4,4096]{1,0:T(4,128)} %get-tuple-element.20), channel_id=1, source_target_pairs={{0,1},{1,2},{2,3},{3,0},{4,5},{5,6},{6,7},{7,4},{8,9},{9,10},{10,1... | collective-permute-start | bytes 196616 | tf_op jit(solution)/shard_map/ppermute | solution.py:400
  33.5 2.4 %collective-permute-start.6 = (f32[4,4096]{1,0:T(4,128)}, f32[4,4096]{1,0:T(4,128)S(1)}, u32[]{:S(2)}, u32[]{:S(2)}) collective-permute-start(f32[4,4096]{1,0:T(4,128)} %get-tuple-element.19), channel_id=1, source_target_pairs={{0,2},{1,3},{2,0},{3,1},{4,6},{5,7},{6,4},{7,5},{8,10},{9,11},{10,... | collective-permute-start | bytes 196616 | tf_op jit(solution)/shard_map/ppermute | solution.py:400
  35.9 1.6 %collective-permute-start.5 = (f32[4,4096]{1,0:T(4,128)S(1)}, f32[4,4096]{1,0:T(4,128)S(1)}, u32[]{:S(2)}, u32[]{:S(2)}) collective-permute-start(f32[4,4096]{1,0:T(4,128)S(1)} %get-tuple-element.18), channel_id=1, source_target_pairs={{0,3},{1,0},{2,1},{3,2},{4,7},{5,4},{6,5},{7,6},{8,11},{9,8},{10,9... | collective-permute-start | bytes 196616 | tf_op jit(solution)/shard_map/ppermute | solution.py:400
  37.4 0.0 all-to-all-done.refs_0_
  37.4 0.0 copy-done.1
  37.4 0.0 copy-done.2
  37.5 0.0 copy-done.5
  37.5 0.0 copy-done.7
  37.5 0.0 copy-start.3
  37.5 0.9 %copy-done.3 = f32[32,2048]{1,0:T(8,128)S(1)} copy-done((f32[32,2048]{1,0:T(8,128)S(1)}, f32[32,2048]{1,0:T(8,128)}, u32[]{:S(2)}) %copy-start.3) | copy-done | bytes 262168
  38.4 4.5 %far.1 = f32[4,4096]{1,0:T(4,128)S(1)} custom-call(f32[64,16,128]{2,1,0:T(8,128)S(1)} %all-to-all-done.refs_0_, s32[8,8]{1,0:T(8,128)S(1)} %copy-done.7, s32[16,64]{1,0:T(8,128)S(1)} %bitcast.5, f32[8,32,256]{2,1,0:T(8,128)S(1)} %copy-done.2, f32[32,2048]{1,0:T(8,128)S(1)} %copy-done.3, f32[16,32,2048]{2,1,0:T(8,128)} %refs_5_.1, f32[32,4096]{1,0:T(8,128)S(1)} %copy-done.1), custom_call_target="tpu_custom_call" | custom-call | flops 4000000000 | tf_op jit(solution)/shard_map/far/pallas_call | solution.py:411
  42.9 0.0 collective-permute-done.7
  42.9 0.0 collective-permute-done.6
  42.9 0.0 collective-permute-done.5
  43.0 0.7 %add_add_fusion = f32[4,4096]{1,0:T(4,128)} fusion(f32[4,4096]{1,0:T(4,128)S(1)} %far.1, f32[4,4096]{1,0:T(4,128)S(1)} %collective-permute-done.7, f32[4,4096]{1,0:T(4,128)S(1)} %collective-permute-done.6, f32[4,4096]{1,0:T(4,128)S(1)} %get-tuple-element.17, f32[4,4096]{1,0:T(4,128)S(1)} %collective-permute-done.5), kind=kLoop, calls=%fused_computation | loop fusion | flops 65536 | bytes 393216 | tf_op jit(solution)/shard_map/add | solution.py:425
Async XLA Ops:
  0.0 18.1 %collective-permute-start = (f32[4,4096]{1,0:T(4,128)}, f32[4,4096]{1,0:T(4,128)S(1)}, u32[]{:S(2)}, u32[]{:S(2)}) collective-permute-start(f32[4,4096]{1,0:T(4,128)} %own_ref.1), channel_id=1, source_target_pairs={{0,4},{4,8},{8,12},{12,16},{16,20},{20,24},{24,28},{28,32},{32,36}... | collective-permute-start | bytes 196616 | tf_op jit(solution)/shard_map/ppermute | solution.py:354
  0.0 18.1 %collective-permute-start.1 = (f32[4,4096]{1,0:T(4,128)}, f32[4,4096]{1,0:T(4,128)S(1)}, u32[]{:S(2)}, u32[]{:S(2)}) collective-permute-start(f32[4,4096]{1,0:T(4,128)} %own_ref.1), channel_id=1, source_target_pairs={{4,0},{8,4},{12,8},{16,12},{20,16},{24,20},{28,24},{32,28},{36,32}... | collective-permute-start | bytes 196616 | tf_op jit(solution)/shard_map/ppermute | solution.py:355
  5.2 12.9 %copy-start.4 = (f32[4,4096]{1,0:T(4,128)S(1)}, f32[4,4096]{1,0:T(4,128)}, u32[]{:S(2)}) copy-start(f32[4,4096]{1,0:T(4,128)} %own_ref.1) | copy-start | bytes 196612
  5.2 12.9 %copy-start.6 = (s32[64,8]{0,1:T(8,128)S(1)}, s32[64,8]{0,1:T(8,128)}, u32[]{:S(2)}) copy-start(s32[64,8]{0,1:T(8,128)} %param.14) | copy-start | bytes 6148
  8.0 22.6 %copy-start = (f32[2,64,4096]{2,1,0:T(8,128)S(1)}, f32[2,64,4096]{2,1,0:T(8,128)}, u32[]{:S(2)}) copy-start(f32[2,64,4096]{2,1,0:T(8,128)} %blocks_in.1) | copy-start | bytes 6291460
  8.0 29.4 %all-to-all-start = ((f32[64,16,128]{2,1,0:T(8,128)}), f32[64,16,128]{2,1,0:T(8,128)S(1)}, u32[]{:S(2)}, u32[]{:S(2)}) async-start(f32[64,16,128]{2,1,0:T(8,128)} %up.1), calls=%async_computation | async-start | bytes 1048576 | tf_op jit(solution)/shard_map/all_to_all | solution.py:368
  20.0 6.8 %collective-permute-start.2 = (f32[32,8,128]{2,1,0:T(8,128)S(1)}, f32[32,8,128]{2,1,0:T(8,128)S(1)}, u32[]{:S(2)}, u32[]{:S(2)}) collective-permute-start(f32[32,8,128]{2,1,0:T(8,128)S(1)} %get-tuple-element.14), channel_id=1, source_target_pairs={{0,1},{1,2},{2,3},{3,0},{4,5},{5,6},{6,7},{7,4},{8,9},{9,10},{10,1... | collective-permute-start | bytes 393224 | tf_op jit(solution)/shard_map/ppermute | solution.py:385
  21.6 9.1 %collective-permute-start.3 = (f32[32,8,128]{2,1,0:T(8,128)S(1)}, f32[32,8,128]{2,1,0:T(8,128)S(1)}, u32[]{:S(2)}, u32[]{:S(2)}) collective-permute-start(f32[32,8,128]{2,1,0:T(8,128)S(1)} %get-tuple-element.15), channel_id=1, source_target_pairs={{0,2},{1,3},{2,0},{3,1},{4,6},{5,7},{6,4},{7,5},{8,10},{9,11},{10,... | collective-permute-start | bytes 393224 | tf_op jit(solution)/shard_map/ppermute | solution.py:385
  24.3 6.3 %collective-permute-start.4 = (f32[32,8,128]{2,1,0:T(8,128)S(1)}, f32[32,8,128]{2,1,0:T(8,128)S(1)}, u32[]{:S(2)}, u32[]{:S(2)}) collective-permute-start(f32[32,8,128]{2,1,0:T(8,128)S(1)} %get-tuple-element.16), channel_id=1, source_target_pairs={{0,3},{1,0},{2,1},{3,2},{4,7},{5,4},{6,5},{7,6},{8,11},{9,8},{10,9... | collective-permute-start | bytes 393224 | tf_op jit(solution)/shard_map/ppermute | solution.py:385
  30.7 6.8 %copy-start.1 = (f32[32,4096]{1,0:T(8,128)S(1)}, f32[32,4096]{1,0:T(8,128)}, u32[]{:S(2)}) copy-start(f32[32,4096]{1,0:T(8,128)} %refs_6_.1) | copy-start | bytes 1572868
  30.7 6.8 %copy-start.2 = (f32[8,32,256]{2,1,0:T(8,128)S(1)}, f32[8,32,256]{2,1,0:T(8,128)}, u32[]{:S(2)}) copy-start(f32[8,32,256]{2,1,0:T(8,128)} %refs_3_.1) | copy-start | bytes 786436
  30.7 6.8 %copy-start.5 = (s32[64,16]{0,1:T(8,128)S(1)}, s32[64,16]{0,1:T(8,128)}, u32[]{:S(2)}) copy-start(s32[64,16]{0,1:T(8,128)} %param.22) | copy-start | bytes 12292
  30.7 6.8 %copy-start.7 = (s32[8,8]{1,0:T(8,128)S(1)}, s32[8,8]{1,0:T(8,128)}, u32[]{:S(2)}) copy-start(s32[8,8]{1,0:T(8,128)} %refs_1_.1) | copy-start | bytes 772
  32.1 10.8 %collective-permute-start.7 = (f32[4,4096]{1,0:T(4,128)}, f32[4,4096]{1,0:T(4,128)S(1)}, u32[]{:S(2)}, u32[]{:S(2)}) collective-permute-start(f32[4,4096]{1,0:T(4,128)} %get-tuple-element.20), channel_id=1, source_target_pairs={{0,1},{1,2},{2,3},{3,0},{4,5},{5,6},{6,7},{7,4},{8,9},{9,10},{10,1... | collective-permute-start | bytes 196616 | tf_op jit(solution)/shard_map/ppermute | solution.py:400
  33.5 9.5 %collective-permute-start.6 = (f32[4,4096]{1,0:T(4,128)}, f32[4,4096]{1,0:T(4,128)S(1)}, u32[]{:S(2)}, u32[]{:S(2)}) collective-permute-start(f32[4,4096]{1,0:T(4,128)} %get-tuple-element.19), channel_id=1, source_target_pairs={{0,2},{1,3},{2,0},{3,1},{4,6},{5,7},{6,4},{7,5},{8,10},{9,11},{10,... | collective-permute-start | bytes 196616 | tf_op jit(solution)/shard_map/ppermute | solution.py:400
  35.9 7.1 %collective-permute-start.5 = (f32[4,4096]{1,0:T(4,128)S(1)}, f32[4,4096]{1,0:T(4,128)S(1)}, u32[]{:S(2)}, u32[]{:S(2)}) collective-permute-start(f32[4,4096]{1,0:T(4,128)S(1)} %get-tuple-element.18), channel_id=1, source_target_pairs={{0,3},{1,0},{2,1},{3,2},{4,7},{5,4},{6,5},{7,6},{8,11},{9,8},{10,9... | collective-permute-start | bytes 196616 | tf_op jit(solution)/shard_map/ppermute | solution.py:400
  37.5 1.0 %copy-start.3 = (f32[32,2048]{1,0:T(8,128)S(1)}, f32[32,2048]{1,0:T(8,128)}, u32[]{:S(2)}) copy-start(f32[32,2048]{1,0:T(8,128)} %refs_4_.1) | copy-start | bytes 786436

commit v4 on v3

--- a/solution.py
+++ b/solution.py
@@ -153,21 +153,24 @@
 
 
 def pick_kernel(list_in, own_ref, left_ref, right_ref, *rest):
-    outs, (table, list_ref, sems) = rest[:-3], rest[-3:]
-    copies = fetch((list_in,), (list_ref,), sems)
+    outs, (table, places_ref, list_ref, sems) = rest[:-4], rest[-4:]
     columns, points = own_ref.shape
     leaf_count = points // PTS
     groups = len(outs)
     share = list_ref.shape[0] // groups
-    base = (lax.axis_index("leaf") - 1) * leaf_count
+    blocks = 3 * points // LANES
+    tile = list_in[...] - (lax.axis_index("leaf") - 1) * leaf_count
+    turned = (tile + iota(tile.shape, 0)) & 1
+    places_ref[...] = (tile >> 1) + turned * blocks
+    copies = fetch((places_ref,), (list_ref,), sems)
     me = lax.axis_index("vec")
     for place, ref in enumerate((left_ref, own_ref, right_ref)):
         for b in range(points // LANES):
             tile = ref[:, b * LANES : (b + 1) * LANES]
             tile = jnp.concatenate([tile, tile], axis=0)
             at = place * (points // LANES) + b
-            table[0, at] = tile
-            table[1, at] = pltpu.roll(tile, PTS, 1)
+            table[at] = tile
+            table[blocks + at] = pltpu.roll(tile, PTS, 1)
     lower = iota((2 * columns, LANES), 1) < PTS
     upper_rows = iota((2 * columns, LANES), 0) >= columns
     for copy in copies:
@@ -177,10 +180,8 @@
         for pair in range(leaf_count // 2):
             halves = []
             for t in (2 * pair, 2 * pair + 1):
-                one = list_ref[first, t] - base
-                two = list_ref[first + 1, t] - base
                 halves.append(
-                    jnp.where(lower, table[one & 1, one >> 1], table[1 - (two & 1), two >> 1])
+                    jnp.where(lower, table[list_ref[first, t]], table[list_ref[first + 1, t]])
                 )
             out[pair] = jnp.where(upper_rows, halves[1], halves[0])
 
@@ -215,42 +216,40 @@
 def far_kernel(*refs):
     recv_ref, sources, out_ref, targets, (hot_ref, sems) = (
         refs[0],
-        refs[1:7],
-        refs[7],
-        refs[8:14],
-        refs[14:],
-    )
-    top_ref, slot_ref, top_coupling_ref, down_ref, coupling_ref, basis_ref = targets
+        refs[1:6],
+        refs[6],
+        refs[7:12],
+        refs[12:],
+    )
+    top_ref, slot_ref, top_coupling_ref, down_ref, coupling_ref = targets
     coupling_in = sources[4]
-    columns, points = out_ref.shape
-    leaf_count = points // PTS
+    par_count, rows = out_ref.shape[:2]
+    columns = rows // GROUP
+    leaf_count = par_count * GROUP
     peers = recv_ref.shape[0]
-    par_count = leaf_count // GROUP
     slots = recv_ref.shape[1] - par_count
     far_count = coupling_ref.shape[0]
     top_count = top_coupling_ref.shape[0]
-    narrow, wide = GROUP * RANK, GROUP * PTS
+    narrow = GROUP * RANK
     groups = range(par_count)
 
     def lanes(g, size):
         return slice(g * size, (g + 1) * size)
 
     copies = [
-        pltpu.make_async_copy(sources[i], targets[i], sems.at[i]) for i in (0, 1, 2, 3, 5)
-    ]
-    copies[4:4] = [
+        pltpu.make_async_copy(sources[i], targets[i], sems.at[i]) for i in range(4)
+    ]
+    copies += [
         pltpu.make_async_copy(
             coupling_in.at[:, :, lanes(g, narrow)],
             coupling_ref.at[:, :, lanes(g, narrow)],
-            sems.at[6 + g],
+            sems.at[4 + g],
         )
         for g in groups
     ]
     for copy in copies:
         copy.start()
-    rows = columns * GROUP
     diagonal = iota((rows, narrow), 1) // RANK == iota((rows, narrow), 0) % GROUP
-    diagonal_out = iota((rows, wide), 1) // PTS == iota((rows, wide), 0) % GROUP
 
     copies[0].wait()
     copies[1].wait()
@@ -292,7 +291,6 @@
                 coupling_ref[:, :, lanes(g, narrow)].reshape(far_count * RANK, narrow),
             )
         )
-    spread = []
     for g in groups:
         above = jnp.concatenate(
             [
@@ -303,20 +301,30 @@
             ],
             axis=0,
         )
-        spread.append(fold(jnp.where(diagonal, fields[g] + above, 0.0))[:, :RANK])
-    for copy in copies[4 + par_count :]:
-        copy.wait()
-    values = [dot3(spread[g], basis_ref[:, lanes(g, wide)]) for g in groups]
-    for g in groups:
-        value = jnp.where(diagonal_out, values[g], 0.0)
-        out_ref[:, lanes(g, wide)] = jnp.sum(value.reshape(columns, GROUP, wide), axis=1)
+        out_ref[g] = fold(jnp.where(diagonal, fields[g] + above, 0.0))
+
+
+def out_kernel(field_ref, basis_ref, *rest):
+    sums, out_ref = rest[:-1], rest[-1]
+    columns = out_ref.shape[0]
+    par_count, rows = field_ref.shape[:2]
+    wide = GROUP * PTS
+    diagonal = iota((rows, wide), 1) // PTS == iota((rows, wide), 0) % GROUP
+    for g in range(par_count):
+        lanes = slice(g * wide, (g + 1) * wide)
+        value = dot3(field_ref[g, :, :RANK], basis_ref[:, lanes])
+        value = jnp.where(diagonal, value, 0.0)
+        total = jnp.sum(value.reshape(columns, GROUP, wide), axis=1)
+        for part in sums:
+            total = total + part[:, lanes]
+        out_ref[:, lanes] = total
 
 
 VMEM = pl.BlockSpec(memory_space=pltpu.VMEM)
 ANY = pl.BlockSpec(memory_space=pl.ANY)
 MIB = 1024 * 1024
-UP_MIB, PICK_MIB, NEAR_MIB, FAR_MIB = 60, 24, 24, 51
-UP_US, PICK_US, NEAR_US, FAR_US = 2, 2, 8, 4
+UP_MIB, PICK_MIB, NEAR_MIB, FAR_MIB, OUT_MIB = 60, 24, 24, 51, 24
+UP_US, PICK_US, NEAR_US, FAR_US, OUT_US = 2, 2, 8, 4, 1
 
 
 def cost(micros):
@@ -371,10 +379,11 @@
         pick_kernel,
         name="pick",
         out_shape=[jax.ShapeDtypeStruct((leaf_count // 2, 2 * columns, LANES), F32)] * groups,
-        in_specs=[ANY] + [VMEM] * 3,
+        in_specs=[VMEM] * 4,
         out_specs=[VMEM] * groups,
         scratch_shapes=[
-            pltpu.VMEM((2, 3 * points // LANES, 2 * columns, LANES), F32),
+            pltpu.VMEM((2 * 3 * points // LANES, 2 * columns, LANES), F32),
+            pltpu.VMEM(near_list.T.shape, jnp.int32),
             pltpu.SMEM(near_list.T.shape, jnp.int32),
             pltpu.SemaphoreType.DMA((1,)),
         ],
@@ -406,12 +415,11 @@
         top_coupling,
         down_transfer,
         leaf_coupling,
-        out_basis,
-    ]
-    far = pl.pallas_call(
+    ]
+    fields = pl.pallas_call(
         far_kernel,
         name="far",
-        out_shape=jax.ShapeDtypeStruct((columns, points), F32),
+        out_shape=jax.ShapeDtypeStruct((par_count, columns * GROUP, LANES), F32),
         in_specs=[VMEM] + [ANY] * len(far_args),
         out_specs=VMEM,
         scratch_shapes=[pltpu.VMEM(array.shape, array.dtype) for array in far_args]
@@ -422,7 +430,15 @@
         compiler_params=pltpu.CompilerParams(vmem_limit_bytes=FAR_MIB * MIB),
         cost_estimate=cost(FAR_US),
     )(recv, *far_args)
-    return far + sum(sums[1:], sums[0])
+    return pl.pallas_call(
+        out_kernel,
+        name="out",
+        out_shape=jax.ShapeDtypeStruct((columns, points), F32),
+        in_specs=[VMEM] * (2 + groups),
+        out_specs=VMEM,
+        compiler_params=pltpu.CompilerParams(vmem_limit_bytes=OUT_MIB * MIB),
+        cost_estimate=cost(OUT_US),
+    )(fields, out_basis, *sums)
 
 
 def solution(mesh):

time: 43.8 us -> 41.8 us (0.954)
  the two profiles are of different devices: /device:TPU:8 before, /device:TPU:1 now
where the time goes in v4:
time: 41.8 us; the launch traced here: 41.6 us
  starting transfers between devices  24.2 us (58%)
  Pallas kernels  9.87 us (24%)
  waiting for transfers between devices  7.33 us (18%)
    all_to_all x1, starting transfers between devices, local(): recv = lax.all_to_all(send, 'leaf', split_axis=0, concat_axis=0, tiled=True)  13 us
    ppermute x3, starting transfers between devices, local(): lax.ppermute(picked[s], 'vec', [(i, (i + s) % groups) for i in range(grou...  4.89 us
    ppermute x3, waiting for transfers between devices, local(): lax.ppermute(picked[s], 'vec', [(i, (i + s) % groups) for i in range(grou...  4.81 us
    pallas_call x1, Pallas kernels, local(): pl.pallas_call(far_kernel, name='far', out_shape=jax.ShapeDtypeStruct((pa...  4.05 us
    ppermute x1, starting transfers between devices, local(): lax.ppermute(points_x, 'leaf', [(i, (i + 1) % ring) for i in range(ring)])  3.03 us
    ppermute x3, starting transfers between devices, local(): lax.ppermute(partial[s], 'vec', [(i, (i - s) % groups) for i in range(gro...  3.02 us
    pallas_call x1, Pallas kernels, local(): pl.pallas_call(up_kernel, name='up', out_shape=jax.ShapeDtypeStruct((peer...  2.83 us
    all_to_all x1, waiting for transfers between devices, local(): recv = lax.all_to_all(send, 'leaf', split_axis=0, concat_axis=0, tiled=True)  2.51 us
  transfers between devices with their start and end apart: 9, of which 3 were waited for; matrix products, arithmetic and copies ran while one was open for 0% of the time, Pallas kernels for 21%

profile of v4, /device:TPU:1, one launch (start us, length us, event | category | flops | bytes accessed | tf_op | source)
XLA Modules:
  0.0 41.6 jit_solution(179693256527685822)
XLA Ops:
  0.0 3.0 %collective-permute-start = (f32[4,4096]{1,0:T(4,128)}, f32[4,4096]{1,0:T(4,128)S(1)}, u32[]{:S(2)}, u32[]{:S(2)}) collective-permute-start(f32[4,4096]{1,0:T(4,128)} %own_ref.1), channel_id=1, source_target_pairs={{0,4},{4,8},{8,12},{12,16},{16,20},{20,24},{24,28},{28,32},{32,36}... | collective-permute-start | bytes 196616 | tf_op jit(solution)/shard_map/ppermute | solution.py:362
  3.0 0.2 collective-permute-start.1
  3.2 0.0 copy-start.4
  3.2 0.0 copy-start.6
  3.2 2.8 %up.1 = f32[64,16,128]{2,1,0:T(8,128)} custom-call(f32[4,4096]{1,0:T(4,128)} %own_ref.1, f32[32,4096]{1,0:T(8,128)} %basis_in.1, f32[32,2048]{1,0:T(8,128)} %up_in.1, s32[8,64]{1,0:T(8,128)} %bitcast.7, s32[1,64]{1,0:T(1,128)} %counts_in.1), custom_call_target="tpu_custom_call" | custom-call | flops 2000000000 | tf_op jit(solution)/shard_map/up/pallas_call | solution.py:366
  6.1 0.0 copy-start
  6.1 13.0 %all-to-all-start = ((f32[64,16,128]{2,1,0:T(8,128)}), f32[64,16,128]{2,1,0:T(8,128)S(1)}, u32[]{:S(2)}, u32[]{:S(2)}) async-start(f32[64,16,128]{2,1,0:T(8,128)} %up.1), calls=%async_computation | async-start | bytes 1048576 | tf_op jit(solution)/shard_map/all_to_all | solution.py:376
  19.1 0.0 collective-permute-done.left_ref
  19.1 0.0 collective-permute-done.1.right_ref
  19.1 0.0 copy-done.4
  19.2 0.0 copy-done.6
  19.2 1.3 %pick.1 = (f32[32,8,128]{2,1,0:T(8,128)S(1)}, f32[32,8,128]{2,1,0:T(8,128)S(1)}, f32[32,8,128]{2,1,0:T(8,128)S(1)}, f32[32,8,128]{2,1,0:T(8,128)S(1)}) custom-call(s32[8,64]{1,0:T(8,128)S(1)} %bitcast.6, f32[4,4096]{1,0:T(4,128)S(1)} %copy-done.4, f32[4,4096]{1,0:T(4,128)S(1)} %collective-permute-done.left_ref, f32[4,4096]{1,0:T(4,128)S(1)} %collective-permute-done.1.right_ref), custom_call_target="tpu_custom_call" | custom-call | flops 2000000000 | tf_op jit(solution)/shard_map/pick/pallas_call | solution.py:378
  20.4 1.3 %collective-permute-start.2 = (f32[32,8,128]{2,1,0:T(8,128)S(1)}, f32[32,8,128]{2,1,0:T(8,128)S(1)}, u32[]{:S(2)}, u32[]{:S(2)}) collective-permute-start(f32[32,8,128]{2,1,0:T(8,128)S(1)} %get-tuple-element.14), channel_id=1, source_target_pairs={{0,1},{1,2},{2,3},{3,0},{4,5},{5,6},{6,7},{7,4},{8,9},{9,10},{10,1... | collective-permute-start | bytes 393224 | tf_op jit(solution)/shard_map/ppermute | solution.py:394
  21.7 2.4 %collective-permute-start.3 = (f32[32,8,128]{2,1,0:T(8,128)S(1)}, f32[32,8,128]{2,1,0:T(8,128)S(1)}, u32[]{:S(2)}, u32[]{:S(2)}) collective-permute-start(f32[32,8,128]{2,1,0:T(8,128)S(1)} %get-tuple-element.15), channel_id=1, source_target_pairs={{0,2},{1,3},{2,0},{3,1},{4,6},{5,7},{6,4},{7,5},{8,10},{9,11},{10,... | collective-permute-start | bytes 393224 | tf_op jit(solution)/shard_map/ppermute | solution.py:394
  24.2 1.2 %collective-permute-start.4 = (f32[32,8,128]{2,1,0:T(8,128)S(1)}, f32[32,8,128]{2,1,0:T(8,128)S(1)}, u32[]{:S(2)}, u32[]{:S(2)}) collective-permute-start(f32[32,8,128]{2,1,0:T(8,128)S(1)} %get-tuple-element.16), channel_id=1, source_target_pairs={{0,3},{1,0},{2,1},{3,2},{4,7},{5,4},{6,5},{7,6},{8,11},{9,8},{10,9... | collective-permute-start | bytes 393224 | tf_op jit(solution)/shard_map/ppermute | solution.py:394
  25.3 1.0 %collective-permute-done.2.rest_1_ = f32[32,8,128]{2,1,0:T(8,128)S(1)} collective-permute-done((f32[32,8,128]{2,1,0:T(8,128)S(1)}, f32[32,8,128]{2,1,0:T(8,128)S(1)}, u32[]{:S(2)}, u32[]{:S(2)}) %collective-permute-start.2) | collective-permute-done | bytes 131104 | tf_op jit(solution)/shard_map/ppermute | solution.py:394
  26.3 3.8 %collective-permute-done.3.rest_2_ = f32[32,8,128]{2,1,0:T(8,128)S(1)} collective-permute-done((f32[32,8,128]{2,1,0:T(8,128)S(1)}, f32[32,8,128]{2,1,0:T(8,128)S(1)}, u32[]{:S(2)}, u32[]{:S(2)}) %collective-permute-start.3) | collective-permute-done | bytes 131104 | tf_op jit(solution)/shard_map/ppermute | solution.py:394
  30.1 0.0 collective-permute-done.4.rest_3_
  30.1 0.0 copy-done
  30.1 0.0 copy-start.2
  30.1 0.0 copy-start.3
  30.2 0.0 copy-start.5
  30.2 0.0 copy-start.7
  30.2 0.7 %near.1 = (f32[4,4096]{1,0:T(4,128)S(1)}, f32[4,4096]{1,0:T(4,128)S(1)}, f32[4,4096]{1,0:T(4,128)S(1)}, f32[4,4096]{1,0:T(4,128)S(1)}) custom-call(f32[2,64,4096]{2,1,0:T(8,128)S(1)} %copy-done, f32[32,8,128]{2,1,0:T(8,128)S(1)} %get-tuple-element.13.rest_0_, f32[32,8,128]{2,1,0:T(8,128)S(1)} %collective-permute-done.2.rest_1_, ...), custom_call_target="tpu_custom_call" | custom-call | flops 8000000000 | tf_op jit(solution)/shard_map/near/pallas_call | solution.py:398
  30.9 2.1 %collective-permute-start.5 = (f32[4,4096]{1,0:T(4,128)S(1)}, f32[4,4096]{1,0:T(4,128)S(1)}, u32[]{:S(2)}, u32[]{:S(2)}) collective-permute-start(f32[4,4096]{1,0:T(4,128)S(1)} %get-tuple-element.18), channel_id=1, source_target_pairs={{0,3},{1,0},{2,1},{3,2},{4,7},{5,4},{6,5},{7,6},{8,11},{9,8},{10,9... | collective-permute-start | bytes 196616 | tf_op jit(solution)/shard_map/ppermute | solution.py:409
  33.0 0.8 %collective-permute-start.6 = (f32[4,4096]{1,0:T(4,128)S(1)}, f32[4,4096]{1,0:T(4,128)S(1)}, u32[]{:S(2)}, u32[]{:S(2)}) collective-permute-start(f32[4,4096]{1,0:T(4,128)S(1)} %get-tuple-element.19), channel_id=1, source_target_pairs={{0,2},{1,3},{2,0},{3,1},{4,6},{5,7},{6,4},{7,5},{8,10},{9,11},{10,... | collective-permute-start | bytes 196616 | tf_op jit(solution)/shard_map/ppermute | solution.py:409
  33.9 0.1 collective-permute-start.7
  33.9 2.5 %all-to-all-done.refs_0_ = f32[64,16,128]{2,1,0:T(8,128)S(1)} async-done(((f32[64,16,128]{2,1,0:T(8,128)}), f32[64,16,128]{2,1,0:T(8,128)S(1)}, u32[]{:S(2)}, u32[]{:S(2)}) %all-to-all-start) | async-done | bytes 524320 | tf_op jit(solution)/shard_map/all_to_all | solution.py:376
  36.4 0.0 copy-done.2
  36.4 0.0 copy-done.3
  36.4 0.0 copy-done.5
  36.5 0.0 copy-done.7
  36.5 0.0 copy-start.1
  36.5 4.0 %far.1.field_ref = f32[8,32,128]{2,1,0:T(8,128)S(1)} custom-call(f32[64,16,128]{2,1,0:T(8,128)S(1)} %all-to-all-done.refs_0_, s32[8,8]{1,0:T(8,128)S(1)} %copy-done.7, s32[16,64]{1,0:T(8,128)S(1)} %bitcast.5, f32[8,32,256]{2,1,0:T(8,128)S(1)} %copy-done.2, f32[32,2048]{1,0:T(8,128)S(1)} %copy-done.3, f32[16,32,2048]{2,1,0:T(8,128)} %refs_5_.1), custom_call_target="tpu_custom_call" | custom-call | flops 4000000000 | tf_op jit(solution)/shard_map/far/pallas_call | solution.py:419
  40.5 0.0 collective-permute-done.5.rest_1_
  40.5 0.0 collective-permute-done.6.rest_2_
  40.6 0.0 collective-permute-done.7.rest_3_
  40.6 0.0 copy-done.1
  40.6 1.0 %out.1 = f32[4,4096]{1,0:T(4,128)} custom-call(f32[8,32,128]{2,1,0:T(8,128)S(1)} %far.1.field_ref, f32[32,4096]{1,0:T(8,128)S(1)} %copy-done.1, f32[4,4096]{1,0:T(4,128)S(1)} %get-tuple-element.17.rest_0_, f32[4,4096]{1,0:T(4,128)S(1)} %collective-permute-done.5.rest_1_, f32[4,4096]{1,0:T(4,128)S(1)} %collective-permute-done.6.rest_2_, ...), custom_call_target="tpu_custom_call" | custom-call | flops 1000000000 | tf_op jit(solution)/shard_map/out/pallas_call | solution.py:433
Async XLA Ops:
  0.0 19.1 %collective-permute-start = (f32[4,4096]{1,0:T(4,128)}, f32[4,4096]{1,0:T(4,128)S(1)}, u32[]{:S(2)}, u32[]{:S(2)}) collective-permute-start(f32[4,4096]{1,0:T(4,128)} %own_ref.1), channel_id=1, source_target_pairs={{0,4},{4,8},{8,12},{12,16},{16,20},{20,24},{24,28},{28,32},{32,36}... | collective-permute-start | bytes 196616 | tf_op jit(solution)/shard_map/ppermute | solution.py:362
  3.0 16.1 %collective-permute-start.1 = (f32[4,4096]{1,0:T(4,128)}, f32[4,4096]{1,0:T(4,128)S(1)}, u32[]{:S(2)}, u32[]{:S(2)}) collective-permute-start(f32[4,4096]{1,0:T(4,128)} %own_ref.1), channel_id=1, source_target_pairs={{4,0},{8,4},{12,8},{16,12},{20,16},{24,20},{28,24},{32,28},{36,32}... | collective-permute-start | bytes 196616 | tf_op jit(solution)/shard_map/ppermute | solution.py:363
  3.2 15.9 %copy-start.4 = (f32[4,4096]{1,0:T(4,128)S(1)}, f32[4,4096]{1,0:T(4,128)}, u32[]{:S(2)}) copy-start(f32[4,4096]{1,0:T(4,128)} %own_ref.1) | copy-start | bytes 196612
  3.2 15.9 %copy-start.6 = (s32[64,8]{0,1:T(8,128)S(1)}, s32[64,8]{0,1:T(8,128)}, u32[]{:S(2)}) copy-start(s32[64,8]{0,1:T(8,128)} %param.14) | copy-start | bytes 6148
  6.1 24.0 %copy-start = (f32[2,64,4096]{2,1,0:T(8,128)S(1)}, f32[2,64,4096]{2,1,0:T(8,128)}, u32[]{:S(2)}) copy-start(f32[2,64,4096]{2,1,0:T(8,128)} %blocks_in.1) | copy-start | bytes 6291460
  6.1 30.3 %all-to-all-start = ((f32[64,16,128]{2,1,0:T(8,128)}), f32[64,16,128]{2,1,0:T(8,128)S(1)}, u32[]{:S(2)}, u32[]{:S(2)}) async-start(f32[64,16,128]{2,1,0:T(8,128)} %up.1), calls=%async_computation | async-start | bytes 1048576 | tf_op jit(solution)/shard_map/all_to_all | solution.py:376
  20.4 5.9 %collective-permute-start.2 = (f32[32,8,128]{2,1,0:T(8,128)S(1)}, f32[32,8,128]{2,1,0:T(8,128)S(1)}, u32[]{:S(2)}, u32[]{:S(2)}) collective-permute-start(f32[32,8,128]{2,1,0:T(8,128)S(1)} %get-tuple-element.14), channel_id=1, source_target_pairs={{0,1},{1,2},{2,3},{3,0},{4,5},{5,6},{6,7},{7,4},{8,9},{9,10},{10,1... | collective-permute-start | bytes 393224 | tf_op jit(solution)/shard_map/ppermute | solution.py:394
  21.7 8.4 %collective-permute-start.3 = (f32[32,8,128]{2,1,0:T(8,128)S(1)}, f32[32,8,128]{2,1,0:T(8,128)S(1)}, u32[]{:S(2)}, u32[]{:S(2)}) collective-permute-start(f32[32,8,128]{2,1,0:T(8,128)S(1)} %get-tuple-element.15), channel_id=1, source_target_pairs={{0,2},{1,3},{2,0},{3,1},{4,6},{5,7},{6,4},{7,5},{8,10},{9,11},{10,... | collective-permute-start | bytes 393224 | tf_op jit(solution)/shard_map/ppermute | solution.py:394
  24.2 6.0 %collective-permute-start.4 = (f32[32,8,128]{2,1,0:T(8,128)S(1)}, f32[32,8,128]{2,1,0:T(8,128)S(1)}, u32[]{:S(2)}, u32[]{:S(2)}) collective-permute-start(f32[32,8,128]{2,1,0:T(8,128)S(1)} %get-tuple-element.16), channel_id=1, source_target_pairs={{0,3},{1,0},{2,1},{3,2},{4,7},{5,4},{6,5},{7,6},{8,11},{9,8},{10,9... | collective-permute-start | bytes 393224 | tf_op jit(solution)/shard_map/ppermute | solution.py:394
  30.1 6.3 %copy-start.2 = (f32[8,32,256]{2,1,0:T(8,128)S(1)}, f32[8,32,256]{2,1,0:T(8,128)}, u32[]{:S(2)}) copy-start(f32[8,32,256]{2,1,0:T(8,128)} %refs_3_.1) | copy-start | bytes 786436
  30.1 6.3 %copy-start.3 = (f32[32,2048]{1,0:T(8,128)S(1)}, f32[32,2048]{1,0:T(8,128)}, u32[]{:S(2)}) copy-start(f32[32,2048]{1,0:T(8,128)} %refs_4_.1) | copy-start | bytes 786436
  30.2 6.3 %copy-start.5 = (s32[64,16]{0,1:T(8,128)S(1)}, s32[64,16]{0,1:T(8,128)}, u32[]{:S(2)}) copy-start(s32[64,16]{0,1:T(8,128)} %param.22) | copy-start | bytes 12292
  30.2 6.3 %copy-start.7 = (s32[8,8]{1,0:T(8,128)S(1)}, s32[8,8]{1,0:T(8,128)}, u32[]{:S(2)}) copy-start(s32[8,8]{1,0:T(8,128)} %refs_1_.1) | copy-start | bytes 772
  30.9 9.6 %collective-permute-start.5 = (f32[4,4096]{1,0:T(4,128)S(1)}, f32[4,4096]{1,0:T(4,128)S(1)}, u32[]{:S(2)}, u32[]{:S(2)}) collective-permute-start(f32[4,4096]{1,0:T(4,128)S(1)} %get-tuple-element.18), channel_id=1, source_target_pairs={{0,3},{1,0},{2,1},{3,2},{4,7},{5,4},{6,5},{7,6},{8,11},{9,8},{10,9... | collective-permute-start | bytes 196616 | tf_op jit(solution)/shard_map/ppermute | solution.py:409
  33.0 7.5 %collective-permute-start.6 = (f32[4,4096]{1,0:T(4,128)S(1)}, f32[4,4096]{1,0:T(4,128)S(1)}, u32[]{:S(2)}, u32[]{:S(2)}) collective-permute-start(f32[4,4096]{1,0:T(4,128)S(1)} %get-tuple-element.19), channel_id=1, source_target_pairs={{0,2},{1,3},{2,0},{3,1},{4,6},{5,7},{6,4},{7,5},{8,10},{9,11},{10,... | collective-permute-start | bytes 196616 | tf_op jit(solution)/shard_map/ppermute | solution.py:409
  33.9 6.7 %collective-permute-start.7 = (f32[4,4096]{1,0:T(4,128)S(1)}, f32[4,4096]{1,0:T(4,128)S(1)}, u32[]{:S(2)}, u32[]{:S(2)}) collective-permute-start(f32[4,4096]{1,0:T(4,128)S(1)} %get-tuple-element.20), channel_id=1, source_target_pairs={{0,1},{1,2},{2,3},{3,0},{4,5},{5,6},{6,7},{7,4},{8,9},{9,10},{10,1... | collective-permute-start | bytes 196616 | tf_op jit(solution)/shard_map/ppermute | solution.py:409
  36.5 4.1 %copy-start.1 = (f32[32,4096]{1,0:T(8,128)S(1)}, f32[32,4096]{1,0:T(8,128)}, u32[]{:S(2)}) copy-start(f32[32,4096]{1,0:T(8,128)} %basis_ref.1) | copy-start | bytes 1572868

commit v5 on v4

--- a/solution.py
+++ b/solution.py
@@ -241,11 +241,11 @@
     ]
     copies += [
         pltpu.make_async_copy(
-            coupling_in.at[:, :, lanes(g, narrow)],
-            coupling_ref.at[:, :, lanes(g, narrow)],
+            coupling_in.at[:, :, lanes(g, 2 * narrow)],
+            coupling_ref.at[:, :, lanes(g, 2 * narrow)],
             sems.at[4 + g],
         )
-        for g in groups
+        for g in range(par_count // 2)
     ]
     for copy in copies:
         copy.start()
@@ -284,7 +284,8 @@
     ]
     fields = []
     for g in groups:
-        copies[4 + g].wait()
+        if g % 2 == 0:
+            copies[4 + g // 2].wait()
         fields.append(
             dot3(
                 gathered[g],

time: 41.8 us -> 40.9 us (0.978)
  the two profiles are of different devices: /device:TPU:1 before, /device:TPU:8 now
where the time goes in v5:
time: 40.9 us; the launch traced here: 40.7 us
  starting transfers between devices  25.1 us (61%)
  Pallas kernels  9.04 us (22%)
  waiting for transfers between devices  6.42 us (16%)
    all_to_all x1, starting transfers between devices, local(): recv = lax.all_to_all(send, 'leaf', split_axis=0, concat_axis=0, tiled=True)  10 us
    ppermute x3, starting transfers between devices, local(): lax.ppermute(picked[s], 'vec', [(i, (i + s) % groups) for i in range(grou...  5.73 us
    ppermute x1, starting transfers between devices, local(): lax.ppermute(points_x, 'leaf', [((i + 1) % ring, i) for i in range(ring)])  5.18 us
    ppermute x3, waiting for transfers between devices, local(): lax.ppermute(picked[s], 'vec', [(i, (i + s) % groups) for i in range(grou...  4.9 us
    ppermute x3, starting transfers between devices, local(): lax.ppermute(partial[s], 'vec', [(i, (i - s) % groups) for i in range(gro...  4.14 us
    pallas_call x1, Pallas kernels, local(): pl.pallas_call(far_kernel, name='far', out_shape=jax.ShapeDtypeStruct((pa...  3.23 us
    pallas_call x1, Pallas kernels, local(): pl.pallas_call(up_kernel, name='up', out_shape=jax.ShapeDtypeStruct((peer...  2.83 us
    ppermute x3, waiting for transfers between devices, local(): lax.ppermute(partial[s], 'vec', [(i, (i - s) % groups) for i in range(gro...  1.51 us
  transfers between devices with their start and end apart: 9, of which 4 were waited for; matrix products, arithmetic and copies ran while one was open for 0% of the time, Pallas kernels for 20%

profile of v5, /device:TPU:8, one launch (start us, length us, event | category | flops | bytes accessed | tf_op | source)
XLA Modules:
  0.0 40.7 jit_solution(17972534257048692732)
XLA Ops:
  0.0 0.0 collective-permute-start
  0.0 5.2 %collective-permute-start.1 = (f32[4,4096]{1,0:T(4,128)}, f32[4,4096]{1,0:T(4,128)S(1)}, u32[]{:S(2)}, u32[]{:S(2)}) collective-permute-start(f32[4,4096]{1,0:T(4,128)} %own_ref.1), channel_id=1, source_target_pairs={{4,0},{8,4},{12,8},{16,12},{20,16},{24,20},{28,24},{32,28},{36,32}... | collective-permute-start | bytes 196616 | tf_op jit(solution)/shard_map/ppermute | solution.py:364
  5.2 0.0 copy-start.4
  5.2 0.0 copy-start.6
  5.2 2.8 %up.1 = f32[64,16,128]{2,1,0:T(8,128)} custom-call(f32[4,4096]{1,0:T(4,128)} %own_ref.1, f32[32,4096]{1,0:T(8,128)} %basis_in.1, f32[32,2048]{1,0:T(8,128)} %up_in.1, s32[8,64]{1,0:T(8,128)} %bitcast.7, s32[1,64]{1,0:T(1,128)} %counts_in.1), custom_call_target="tpu_custom_call" | custom-call | flops 2000000000 | tf_op jit(solution)/shard_map/up/pallas_call | solution.py:367
  8.0 0.0 copy-start
  8.0 10.0 %all-to-all-start = ((f32[64,16,128]{2,1,0:T(8,128)}), f32[64,16,128]{2,1,0:T(8,128)S(1)}, u32[]{:S(2)}, u32[]{:S(2)}) async-start(f32[64,16,128]{2,1,0:T(8,128)} %up.1), calls=%async_computation | async-start | bytes 1048576 | tf_op jit(solution)/shard_map/all_to_all | solution.py:377
  18.1 0.0 collective-permute-done.left_ref
  18.1 0.0 collective-permute-done.1.right_ref
  18.1 0.0 copy-done.4
  18.1 0.0 copy-done.6
  18.1 1.3 %pick.1 = (f32[32,8,128]{2,1,0:T(8,128)S(1)}, f32[32,8,128]{2,1,0:T(8,128)S(1)}, f32[32,8,128]{2,1,0:T(8,128)S(1)}, f32[32,8,128]{2,1,0:T(8,128)S(1)}) custom-call(s32[8,64]{1,0:T(8,128)S(1)} %bitcast.6, f32[4,4096]{1,0:T(4,128)S(1)} %copy-done.4, f32[4,4096]{1,0:T(4,128)S(1)} %collective-permute-done.left_ref, f32[4,4096]{1,0:T(4,128)S(1)} %collective-permute-done.1.right_ref), custom_call_target="tpu_custom_call" | custom-call | flops 2000000000 | tf_op jit(solution)/shard_map/pick/pallas_call | solution.py:379
  19.4 1.6 %collective-permute-start.2 = (f32[32,8,128]{2,1,0:T(8,128)S(1)}, f32[32,8,128]{2,1,0:T(8,128)S(1)}, u32[]{:S(2)}, u32[]{:S(2)}) collective-permute-start(f32[32,8,128]{2,1,0:T(8,128)S(1)} %get-tuple-element.14), channel_id=1, source_target_pairs={{0,1},{1,2},{2,3},{3,0},{4,5},{5,6},{6,7},{7,4},{8,9},{9,10},{10,1... | collective-permute-start | bytes 393224 | tf_op jit(solution)/shard_map/ppermute | solution.py:395
  21.0 2.7 %collective-permute-start.3 = (f32[32,8,128]{2,1,0:T(8,128)S(1)}, f32[32,8,128]{2,1,0:T(8,128)S(1)}, u32[]{:S(2)}, u32[]{:S(2)}) collective-permute-start(f32[32,8,128]{2,1,0:T(8,128)S(1)} %get-tuple-element.15), channel_id=1, source_target_pairs={{0,2},{1,3},{2,0},{3,1},{4,6},{5,7},{6,4},{7,5},{8,10},{9,11},{10,... | collective-permute-start | bytes 393224 | tf_op jit(solution)/shard_map/ppermute | solution.py:395
  23.7 1.4 %collective-permute-start.4 = (f32[32,8,128]{2,1,0:T(8,128)S(1)}, f32[32,8,128]{2,1,0:T(8,128)S(1)}, u32[]{:S(2)}, u32[]{:S(2)}) collective-permute-start(f32[32,8,128]{2,1,0:T(8,128)S(1)} %get-tuple-element.16), channel_id=1, source_target_pairs={{0,3},{1,0},{2,1},{3,2},{4,7},{5,4},{6,5},{7,6},{8,11},{9,8},{10,9... | collective-permute-start | bytes 393224 | tf_op jit(solution)/shard_map/ppermute | solution.py:395
  25.1 1.1 %collective-permute-done.2.rest_1_ = f32[32,8,128]{2,1,0:T(8,128)S(1)} collective-permute-done((f32[32,8,128]{2,1,0:T(8,128)S(1)}, f32[32,8,128]{2,1,0:T(8,128)S(1)}, u32[]{:S(2)}, u32[]{:S(2)}) %collective-permute-start.2) | collective-permute-done | bytes 131104 | tf_op jit(solution)/shard_map/ppermute | solution.py:395
  26.2 3.8 %collective-permute-done.3.rest_2_ = f32[32,8,128]{2,1,0:T(8,128)S(1)} collective-permute-done((f32[32,8,128]{2,1,0:T(8,128)S(1)}, f32[32,8,128]{2,1,0:T(8,128)S(1)}, u32[]{:S(2)}, u32[]{:S(2)}) %collective-permute-start.3) | collective-permute-done | bytes 131104 | tf_op jit(solution)/shard_map/ppermute | solution.py:395
  30.0 0.0 collective-permute-done.4.rest_3_
  30.0 0.0 copy-done
  30.0 0.0 copy-start.2
  30.0 0.0 copy-start.3
  30.0 0.0 copy-start.5
  30.1 0.0 copy-start.7
  30.1 0.7 %near.1 = (f32[4,4096]{1,0:T(4,128)S(1)}, f32[4,4096]{1,0:T(4,128)S(1)}, f32[4,4096]{1,0:T(4,128)S(1)}, f32[4,4096]{1,0:T(4,128)S(1)}) custom-call(f32[2,64,4096]{2,1,0:T(8,128)S(1)} %copy-done, f32[32,8,128]{2,1,0:T(8,128)S(1)} %get-tuple-element.13.rest_0_, f32[32,8,128]{2,1,0:T(8,128)S(1)} %collective-permute-done.2.rest_1_, ...), custom_call_target="tpu_custom_call" | custom-call | flops 8000000000 | tf_op jit(solution)/shard_map/near/pallas_call | solution.py:399
  30.8 2.3 %collective-permute-start.5 = (f32[4,4096]{1,0:T(4,128)S(1)}, f32[4,4096]{1,0:T(4,128)S(1)}, u32[]{:S(2)}, u32[]{:S(2)}) collective-permute-start(f32[4,4096]{1,0:T(4,128)S(1)} %get-tuple-element.18), channel_id=1, source_target_pairs={{0,3},{1,0},{2,1},{3,2},{4,7},{5,4},{6,5},{7,6},{8,11},{9,8},{10,9... | collective-permute-start | bytes 196616 | tf_op jit(solution)/shard_map/ppermute | solution.py:410
  33.1 1.1 %collective-permute-start.6 = (f32[4,4096]{1,0:T(4,128)S(1)}, f32[4,4096]{1,0:T(4,128)S(1)}, u32[]{:S(2)}, u32[]{:S(2)}) collective-permute-start(f32[4,4096]{1,0:T(4,128)S(1)} %get-tuple-element.19), channel_id=1, source_target_pairs={{0,2},{1,3},{2,0},{3,1},{4,6},{5,7},{6,4},{7,5},{8,10},{9,11},{10,... | collective-permute-start | bytes 196616 | tf_op jit(solution)/shard_map/ppermute | solution.py:410
  34.3 0.7 %collective-permute-start.7 = (f32[4,4096]{1,0:T(4,128)S(1)}, f32[4,4096]{1,0:T(4,128)S(1)}, u32[]{:S(2)}, u32[]{:S(2)}) collective-permute-start(f32[4,4096]{1,0:T(4,128)S(1)} %get-tuple-element.20), channel_id=1, source_target_pairs={{0,1},{1,2},{2,3},{3,0},{4,5},{5,6},{6,7},{7,4},{8,9},{9,10},{10,1... | collective-permute-start | bytes 196616 | tf_op jit(solution)/shard_map/ppermute | solution.py:410
  34.9 0.0 all-to-all-done.refs_0_
  34.9 0.0 copy-done.2
  34.9 0.0 copy-done.3
  34.9 0.0 copy-done.5
  35.0 0.0 copy-done.7
  35.0 0.0 copy-start.1
  35.0 3.2 %far.1.field_ref = f32[8,32,128]{2,1,0:T(8,128)S(1)} custom-call(f32[64,16,128]{2,1,0:T(8,128)S(1)} %all-to-all-done.refs_0_, s32[8,8]{1,0:T(8,128)S(1)} %copy-done.7, s32[16,64]{1,0:T(8,128)S(1)} %bitcast.5, f32[8,32,256]{2,1,0:T(8,128)S(1)} %copy-done.2, f32[32,2048]{1,0:T(8,128)S(1)} %copy-done.3, f32[16,32,2048]{2,1,0:T(8,128)} %refs_5_.1), custom_call_target="tpu_custom_call" | custom-call | flops 4000000000 | tf_op jit(solution)/shard_map/far/pallas_call | solution.py:420
  38.2 0.0 collective-permute-done.5.rest_1_
  38.2 0.7 %collective-permute-done.6.rest_2_ = f32[4,4096]{1,0:T(4,128)S(1)} collective-permute-done((f32[4,4096]{1,0:T(4,128)S(1)}, f32[4,4096]{1,0:T(4,128)S(1)}, u32[]{:S(2)}, u32[]{:S(2)}) %collective-permute-start.6) | collective-permute-done | bytes 65568 | tf_op jit(solution)/shard_map/ppermute | solution.py:410
  38.9 0.8 %collective-permute-done.7.rest_3_ = f32[4,4096]{1,0:T(4,128)S(1)} collective-permute-done((f32[4,4096]{1,0:T(4,128)S(1)}, f32[4,4096]{1,0:T(4,128)S(1)}, u32[]{:S(2)}, u32[]{:S(2)}) %collective-permute-start.7) | collective-permute-done | bytes 65568 | tf_op jit(solution)/shard_map/ppermute | solution.py:410
  39.7 0.0 copy-done.1
  39.7 1.0 %out.1 = f32[4,4096]{1,0:T(4,128)} custom-call(f32[8,32,128]{2,1,0:T(8,128)S(1)} %far.1.field_ref, f32[32,4096]{1,0:T(8,128)S(1)} %copy-done.1, f32[4,4096]{1,0:T(4,128)S(1)} %get-tuple-element.17.rest_0_, f32[4,4096]{1,0:T(4,128)S(1)} %collective-permute-done.5.rest_1_, f32[4,4096]{1,0:T(4,128)S(1)} %collective-permute-done.6.rest_2_, ...), custom_call_target="tpu_custom_call" | custom-call | flops 1000000000 | tf_op jit(solution)/shard_map/out/pallas_call | solution.py:434
Async XLA Ops:
  0.0 18.1 %collective-permute-start = (f32[4,4096]{1,0:T(4,128)}, f32[4,4096]{1,0:T(4,128)S(1)}, u32[]{:S(2)}, u32[]{:S(2)}) collective-permute-start(f32[4,4096]{1,0:T(4,128)} %own_ref.1), channel_id=1, source_target_pairs={{0,4},{4,8},{8,12},{12,16},{16,20},{20,24},{24,28},{28,32},{32,36}... | collective-permute-start | bytes 196616 | tf_op jit(solution)/shard_map/ppermute | solution.py:363
  0.0 18.1 %collective-permute-start.1 = (f32[4,4096]{1,0:T(4,128)}, f32[4,4096]{1,0:T(4,128)S(1)}, u32[]{:S(2)}, u32[]{:S(2)}) collective-permute-start(f32[4,4096]{1,0:T(4,128)} %own_ref.1), channel_id=1, source_target_pairs={{4,0},{8,4},{12,8},{16,12},{20,16},{24,20},{28,24},{32,28},{36,32}... | collective-permute-start | bytes 196616 | tf_op jit(solution)/shard_map/ppermute | solution.py:364
  5.2 12.9 %copy-start.4 = (f32[4,4096]{1,0:T(4,128)S(1)}, f32[4,4096]{1,0:T(4,128)}, u32[]{:S(2)}) copy-start(f32[4,4096]{1,0:T(4,128)} %own_ref.1) | copy-start | bytes 196612
  5.2 12.9 %copy-start.6 = (s32[64,8]{0,1:T(8,128)S(1)}, s32[64,8]{0,1:T(8,128)}, u32[]{:S(2)}) copy-start(s32[64,8]{0,1:T(8,128)} %param.14) | copy-start | bytes 6148
  8.0 22.0 %copy-start = (f32[2,64,4096]{2,1,0:T(8,128)S(1)}, f32[2,64,4096]{2,1,0:T(8,128)}, u32[]{:S(2)}) copy-start(f32[2,64,4096]{2,1,0:T(8,128)} %blocks_in.1) | copy-start | bytes 6291460
  8.0 26.9 %all-to-all-start = ((f32[64,16,128]{2,1,0:T(8,128)}), f32[64,16,128]{2,1,0:T(8,128)S(1)}, u32[]{:S(2)}, u32[]{:S(2)}) async-start(f32[64,16,128]{2,1,0:T(8,128)} %up.1), calls=%async_computation | async-start | bytes 1048576 | tf_op jit(solution)/shard_map/all_to_all | solution.py:377
  19.4 6.8 %collective-permute-start.2 = (f32[32,8,128]{2,1,0:T(8,128)S(1)}, f32[32,8,128]{2,1,0:T(8,128)S(1)}, u32[]{:S(2)}, u32[]{:S(2)}) collective-permute-start(f32[32,8,128]{2,1,0:T(8,128)S(1)} %get-tuple-element.14), channel_id=1, source_target_pairs={{0,1},{1,2},{2,3},{3,0},{4,5},{5,6},{6,7},{7,4},{8,9},{9,10},{10,1... | collective-permute-start | bytes 393224 | tf_op jit(solution)/shard_map/ppermute | solution.py:395
  21.0 9.1 %collective-permute-start.3 = (f32[32,8,128]{2,1,0:T(8,128)S(1)}, f32[32,8,128]{2,1,0:T(8,128)S(1)}, u32[]{:S(2)}, u32[]{:S(2)}) collective-permute-start(f32[32,8,128]{2,1,0:T(8,128)S(1)} %get-tuple-element.15), channel_id=1, source_target_pairs={{0,2},{1,3},{2,0},{3,1},{4,6},{5,7},{6,4},{7,5},{8,10},{9,11},{10,... | collective-permute-start | bytes 393224 | tf_op jit(solution)/shard_map/ppermute | solution.py:395
  23.7 6.3 %collective-permute-start.4 = (f32[32,8,128]{2,1,0:T(8,128)S(1)}, f32[32,8,128]{2,1,0:T(8,128)S(1)}, u32[]{:S(2)}, u32[]{:S(2)}) collective-permute-start(f32[32,8,128]{2,1,0:T(8,128)S(1)} %get-tuple-element.16), channel_id=1, source_target_pairs={{0,3},{1,0},{2,1},{3,2},{4,7},{5,4},{6,5},{7,6},{8,11},{9,8},{10,9... | collective-permute-start | bytes 393224 | tf_op jit(solution)/shard_map/ppermute | solution.py:395
  30.0 4.9 %copy-start.2 = (f32[8,32,256]{2,1,0:T(8,128)S(1)}, f32[8,32,256]{2,1,0:T(8,128)}, u32[]{:S(2)}) copy-start(f32[8,32,256]{2,1,0:T(8,128)} %refs_3_.1) | copy-start | bytes 786436
  30.0 4.9 %copy-start.3 = (f32[32,2048]{1,0:T(8,128)S(1)}, f32[32,2048]{1,0:T(8,128)}, u32[]{:S(2)}) copy-start(f32[32,2048]{1,0:T(8,128)} %refs_4_.1) | copy-start | bytes 786436
  30.0 4.9 %copy-start.5 = (s32[64,16]{0,1:T(8,128)S(1)}, s32[64,16]{0,1:T(8,128)}, u32[]{:S(2)}) copy-start(s32[64,16]{0,1:T(8,128)} %param.22) | copy-start | bytes 12292
  30.1 4.9 %copy-start.7 = (s32[8,8]{1,0:T(8,128)S(1)}, s32[8,8]{1,0:T(8,128)}, u32[]{:S(2)}) copy-start(s32[8,8]{1,0:T(8,128)} %refs_1_.1) | copy-start | bytes 772
  30.8 7.4 %collective-permute-start.5 = (f32[4,4096]{1,0:T(4,128)S(1)}, f32[4,4096]{1,0:T(4,128)S(1)}, u32[]{:S(2)}, u32[]{:S(2)}) collective-permute-start(f32[4,4096]{1,0:T(4,128)S(1)} %get-tuple-element.18), channel_id=1, source_target_pairs={{0,3},{1,0},{2,1},{3,2},{4,7},{5,4},{6,5},{7,6},{8,11},{9,8},{10,9... | collective-permute-start | bytes 196616 | tf_op jit(solution)/shard_map/ppermute | solution.py:410
  33.1 5.8 %collective-permute-start.6 = (f32[4,4096]{1,0:T(4,128)S(1)}, f32[4,4096]{1,0:T(4,128)S(1)}, u32[]{:S(2)}, u32[]{:S(2)}) collective-permute-start(f32[4,4096]{1,0:T(4,128)S(1)} %get-tuple-element.19), channel_id=1, source_target_pairs={{0,2},{1,3},{2,0},{3,1},{4,6},{5,7},{6,4},{7,5},{8,10},{9,11},{10,... | collective-permute-start | bytes 196616 | tf_op jit(solution)/shard_map/ppermute | solution.py:410
  34.3 5.5 %collective-permute-start.7 = (f32[4,4096]{1,0:T(4,128)S(1)}, f32[4,4096]{1,0:T(4,128)S(1)}, u32[]{:S(2)}, u32[]{:S(2)}) collective-permute-start(f32[4,4096]{1,0:T(4,128)S(1)} %get-tuple-element.20), channel_id=1, source_target_pairs={{0,1},{1,2},{2,3},{3,0},{4,5},{5,6},{6,7},{7,4},{8,9},{9,10},{10,1... | collective-permute-start | bytes 196616 | tf_op jit(solution)/shard_map/ppermute | solution.py:410
  35.0 4.8 %copy-start.1 = (f32[32,4096]{1,0:T(8,128)S(1)}, f32[32,4096]{1,0:T(8,128)}, u32[]{:S(2)}) copy-start(f32[32,4096]{1,0:T(8,128)} %basis_ref.1) | copy-start | bytes 1572868

commit v6 on v5

--- a/solution.py
+++ b/solution.py
@@ -91,7 +91,13 @@
 
 def up_kernel(x_in, basis_in, up_in, leaves_in, counts_in, send_ref, *scratch):
     x_ref, basis_ref, up_ref, leaves_ref, counts_ref, sems = scratch
-    for copy in fetch((x_in, basis_in, up_in, leaves_in, counts_in), scratch[:5], sems):
+    half = basis_in.shape[1] // 2
+    left, right = (slice(None), slice(0, half)), (slice(None), slice(half, 2 * half))
+    for copy in fetch(
+        (basis_in.at[left], basis_in.at[right], x_in, up_in, leaves_in, counts_in),
+        (basis_ref.at[left], basis_ref.at[right], x_ref, up_ref, leaves_ref, counts_ref),
+        sems,
+    ):
         copy.wait()
     columns = x_ref.shape[0]
     leaf_count = x_ref.shape[1] // PTS
@@ -370,7 +376,7 @@
         out_shape=jax.ShapeDtypeStruct((peers, slots + par_count, LANES), F32),
         in_specs=[ANY] * 5,
         out_specs=VMEM,
-        scratch_shapes=buffers(*up_args),
+        scratch_shapes=buffers(*up_args)[:-1] + [pltpu.SemaphoreType.DMA((len(up_args) + 1,))],
         compiler_params=pltpu.CompilerParams(vmem_limit_bytes=UP_MIB * MIB),
         cost_estimate=cost(UP_US),
     )(*up_args)

time: 40.9 us -> 40.9 us (level)
  no operation moved by 1% of the time
where the time goes in v6:
time: 40.9 us; the launch traced here: 40.7 us
  starting transfers between devices  25.1 us (61%)
  Pallas kernels  9.04 us (22%)
  waiting for transfers between devices  6.42 us (16%)
    all_to_all x1, starting transfers between devices, local(): recv = lax.all_to_all(send, 'leaf', split_axis=0, concat_axis=0, tiled=True)  10 us
    ppermute x3, starting transfers between devices, local(): lax.ppermute(picked[s], 'vec', [(i, (i + s) % groups) for i in range(grou...  5.73 us
    ppermute x1, starting transfers between devices, local(): lax.ppermute(points_x, 'leaf', [((i + 1) % ring, i) for i in range(ring)])  5.18 us
    ppermute x3, waiting for transfers between devices, local(): lax.ppermute(picked[s], 'vec', [(i, (i + s) % groups) for i in range(grou...  4.9 us
    ppermute x3, starting transfers between devices, local(): lax.ppermute(partial[s], 'vec', [(i, (i - s) % groups) for i in range(gro...  4.14 us
    pallas_call x1, Pallas kernels, local(): pl.pallas_call(far_kernel, name='far', out_shape=jax.ShapeDtypeStruct((pa...  3.23 us
    pallas_call x1, Pallas kernels, local(): pl.pallas_call(up_kernel, name='up', out_shape=jax.ShapeDtypeStruct((peer...  2.83 us
    ppermute x3, waiting for transfers between devices, local(): lax.ppermute(partial[s], 'vec', [(i, (i - s) % groups) for i in range(gro...  1.51 us
  transfers between devices with their start and end apart: 9, of which 4 were waited for; matrix products, arithmetic and copies ran while one was open for 0% of the time, Pallas kernels for 20%

profile of v6, /device:TPU:8, one launch (start us, length us, event | category | flops | bytes accessed | tf_op | source)
XLA Modules:
  0.0 40.7 jit_solution(587106829729926392)
XLA Ops:
  0.0 0.0 collective-permute-start
  0.0 5.2 %collective-permute-start.1 = (f32[4,4096]{1,0:T(4,128)}, f32[4,4096]{1,0:T(4,128)S(1)}, u32[]{:S(2)}, u32[]{:S(2)}) collective-permute-start(f32[4,4096]{1,0:T(4,128)} %own_ref.1), channel_id=1, source_target_pairs={{4,0},{8,4},{12,8},{16,12},{20,16},{24,20},{28,24},{32,28},{36,32}... | collective-permute-start | bytes 196616 | tf_op jit(solution)/shard_map/ppermute | solution.py:370
  5.2 0.0 copy-start.4
  5.2 0.0 copy-start.6
  5.2 2.8 %up.1 = f32[64,16,128]{2,1,0:T(8,128)} custom-call(f32[4,4096]{1,0:T(4,128)} %own_ref.1, f32[32,4096]{1,0:T(8,128)} %basis_in.1, f32[32,2048]{1,0:T(8,128)} %up_in.1, s32[8,64]{1,0:T(8,128)} %bitcast.7, s32[1,64]{1,0:T(1,128)} %counts_in.1), custom_call_target="tpu_custom_call" | custom-call | flops 2000000000 | tf_op jit(solution)/shard_map/up/pallas_call | solution.py:373
  8.0 0.0 copy-start
  8.0 10.0 %all-to-all-start = ((f32[64,16,128]{2,1,0:T(8,128)}), f32[64,16,128]{2,1,0:T(8,128)S(1)}, u32[]{:S(2)}, u32[]{:S(2)}) async-start(f32[64,16,128]{2,1,0:T(8,128)} %up.1), calls=%async_computation | async-start | bytes 1048576 | tf_op jit(solution)/shard_map/all_to_all | solution.py:383
  18.1 0.0 collective-permute-done.left_ref
  18.1 0.0 collective-permute-done.1.right_ref
  18.1 0.0 copy-done.4
  18.1 0.0 copy-done.6
  18.1 1.3 %pick.1 = (f32[32,8,128]{2,1,0:T(8,128)S(1)}, f32[32,8,128]{2,1,0:T(8,128)S(1)}, f32[32,8,128]{2,1,0:T(8,128)S(1)}, f32[32,8,128]{2,1,0:T(8,128)S(1)}) custom-call(s32[8,64]{1,0:T(8,128)S(1)} %bitcast.6, f32[4,4096]{1,0:T(4,128)S(1)} %copy-done.4, f32[4,4096]{1,0:T(4,128)S(1)} %collective-permute-done.left_ref, f32[4,4096]{1,0:T(4,128)S(1)} %collective-permute-done.1.right_ref), custom_call_target="tpu_custom_call" | custom-call | flops 2000000000 | tf_op jit(solution)/shard_map/pick/pallas_call | solution.py:385
  19.4 1.6 %collective-permute-start.2 = (f32[32,8,128]{2,1,0:T(8,128)S(1)}, f32[32,8,128]{2,1,0:T(8,128)S(1)}, u32[]{:S(2)}, u32[]{:S(2)}) collective-permute-start(f32[32,8,128]{2,1,0:T(8,128)S(1)} %get-tuple-element.14), channel_id=1, source_target_pairs={{0,1},{1,2},{2,3},{3,0},{4,5},{5,6},{6,7},{7,4},{8,9},{9,10},{10,1... | collective-permute-start | bytes 393224 | tf_op jit(solution)/shard_map/ppermute | solution.py:401
  20.9 2.7 %collective-permute-start.3 = (f32[32,8,128]{2,1,0:T(8,128)S(1)}, f32[32,8,128]{2,1,0:T(8,128)S(1)}, u32[]{:S(2)}, u32[]{:S(2)}) collective-permute-start(f32[32,8,128]{2,1,0:T(8,128)S(1)} %get-tuple-element.15), channel_id=1, source_target_pairs={{0,2},{1,3},{2,0},{3,1},{4,6},{5,7},{6,4},{7,5},{8,10},{9,11},{10,... | collective-permute-start | bytes 393224 | tf_op jit(solution)/shard_map/ppermute | solution.py:401
  23.7 1.4 %collective-permute-start.4 = (f32[32,8,128]{2,1,0:T(8,128)S(1)}, f32[32,8,128]{2,1,0:T(8,128)S(1)}, u32[]{:S(2)}, u32[]{:S(2)}) collective-permute-start(f32[32,8,128]{2,1,0:T(8,128)S(1)} %get-tuple-element.16), channel_id=1, source_target_pairs={{0,3},{1,0},{2,1},{3,2},{4,7},{5,4},{6,5},{7,6},{8,11},{9,8},{10,9... | collective-permute-start | bytes 393224 | tf_op jit(solution)/shard_map/ppermute | solution.py:401
  25.1 1.1 %collective-permute-done.2.rest_1_ = f32[32,8,128]{2,1,0:T(8,128)S(1)} collective-permute-done((f32[32,8,128]{2,1,0:T(8,128)S(1)}, f32[32,8,128]{2,1,0:T(8,128)S(1)}, u32[]{:S(2)}, u32[]{:S(2)}) %collective-permute-start.2) | collective-permute-done | bytes 131104 | tf_op jit(solution)/shard_map/ppermute | solution.py:401
  26.2 3.8 %collective-permute-done.3.rest_2_ = f32[32,8,128]{2,1,0:T(8,128)S(1)} collective-permute-done((f32[32,8,128]{2,1,0:T(8,128)S(1)}, f32[32,8,128]{2,1,0:T(8,128)S(1)}, u32[]{:S(2)}, u32[]{:S(2)}) %collective-permute-start.3) | collective-permute-done | bytes 131104 | tf_op jit(solution)/shard_map/ppermute | solution.py:401
  30.0 0.0 collective-permute-done.4.rest_3_
  30.0 0.0 copy-done
  30.0 0.0 copy-start.2
  30.0 0.0 copy-start.3
  30.0 0.0 copy-start.5
  30.0 0.0 copy-start.7
  30.1 0.7 %near.1 = (f32[4,4096]{1,0:T(4,128)S(1)}, f32[4,4096]{1,0:T(4,128)S(1)}, f32[4,4096]{1,0:T(4,128)S(1)}, f32[4,4096]{1,0:T(4,128)S(1)}) custom-call(f32[2,64,4096]{2,1,0:T(8,128)S(1)} %copy-done, f32[32,8,128]{2,1,0:T(8,128)S(1)} %get-tuple-element.13.rest_0_, f32[32,8,128]{2,1,0:T(8,128)S(1)} %collective-permute-done.2.rest_1_, ...), custom_call_target="tpu_custom_call" | custom-call | flops 8000000000 | tf_op jit(solution)/shard_map/near/pallas_call | solution.py:405
  30.8 2.3 %collective-permute-start.5 = (f32[4,4096]{1,0:T(4,128)S(1)}, f32[4,4096]{1,0:T(4,128)S(1)}, u32[]{:S(2)}, u32[]{:S(2)}) collective-permute-start(f32[4,4096]{1,0:T(4,128)S(1)} %get-tuple-element.18), channel_id=1, source_target_pairs={{0,3},{1,0},{2,1},{3,2},{4,7},{5,4},{6,5},{7,6},{8,11},{9,8},{10,9... | collective-permute-start | bytes 196616 | tf_op jit(solution)/shard_map/ppermute | solution.py:416
  33.1 1.1 %collective-permute-start.6 = (f32[4,4096]{1,0:T(4,128)S(1)}, f32[4,4096]{1,0:T(4,128)S(1)}, u32[]{:S(2)}, u32[]{:S(2)}) collective-permute-start(f32[4,4096]{1,0:T(4,128)S(1)} %get-tuple-element.19), channel_id=1, source_target_pairs={{0,2},{1,3},{2,0},{3,1},{4,6},{5,7},{6,4},{7,5},{8,10},{9,11},{10,... | collective-permute-start | bytes 196616 | tf_op jit(solution)/shard_map/ppermute | solution.py:416
  34.3 0.7 %collective-permute-start.7 = (f32[4,4096]{1,0:T(4,128)S(1)}, f32[4,4096]{1,0:T(4,128)S(1)}, u32[]{:S(2)}, u32[]{:S(2)}) collective-permute-start(f32[4,4096]{1,0:T(4,128)S(1)} %get-tuple-element.20), channel_id=1, source_target_pairs={{0,1},{1,2},{2,3},{3,0},{4,5},{5,6},{6,7},{7,4},{8,9},{9,10},{10,1... | collective-permute-start | bytes 196616 | tf_op jit(solution)/shard_map/ppermute | solution.py:416
  34.9 0.0 all-to-all-done.refs_0_
  34.9 0.0 copy-done.2
  34.9 0.0 copy-done.3
  34.9 0.0 copy-done.5
  35.0 0.0 copy-done.7
  35.0 0.0 copy-start.1
  35.0 3.2 %far.1.field_ref = f32[8,32,128]{2,1,0:T(8,128)S(1)} custom-call(f32[64,16,128]{2,1,0:T(8,128)S(1)} %all-to-all-done.refs_0_, s32[8,8]{1,0:T(8,128)S(1)} %copy-done.7, s32[16,64]{1,0:T(8,128)S(1)} %bitcast.5, f32[8,32,256]{2,1,0:T(8,128)S(1)} %copy-done.2, f32[32,2048]{1,0:T(8,128)S(1)} %copy-done.3, f32[16,32,2048]{2,1,0:T(8,128)} %refs_5_.1), custom_call_target="tpu_custom_call" | custom-call | flops 4000000000 | tf_op jit(solution)/shard_map/far/pallas_call | solution.py:426
  38.2 0.0 collective-permute-done.5.rest_1_
  38.2 0.7 %collective-permute-done.6.rest_2_ = f32[4,4096]{1,0:T(4,128)S(1)} collective-permute-done((f32[4,4096]{1,0:T(4,128)S(1)}, f32[4,4096]{1,0:T(4,128)S(1)}, u32[]{:S(2)}, u32[]{:S(2)}) %collective-permute-start.6) | collective-permute-done | bytes 65568 | tf_op jit(solution)/shard_map/ppermute | solution.py:416
  38.9 0.8 %collective-permute-done.7.rest_3_ = f32[4,4096]{1,0:T(4,128)S(1)} collective-permute-done((f32[4,4096]{1,0:T(4,128)S(1)}, f32[4,4096]{1,0:T(4,128)S(1)}, u32[]{:S(2)}, u32[]{:S(2)}) %collective-permute-start.7) | collective-permute-done | bytes 65568 | tf_op jit(solution)/shard_map/ppermute | solution.py:416
  39.7 0.0 copy-done.1
  39.7 1.0 %out.1 = f32[4,4096]{1,0:T(4,128)} custom-call(f32[8,32,128]{2,1,0:T(8,128)S(1)} %far.1.field_ref, f32[32,4096]{1,0:T(8,128)S(1)} %copy-done.1, f32[4,4096]{1,0:T(4,128)S(1)} %get-tuple-element.17.rest_0_, f32[4,4096]{1,0:T(4,128)S(1)} %collective-permute-done.5.rest_1_, f32[4,4096]{1,0:T(4,128)S(1)} %collective-permute-done.6.rest_2_, ...), custom_call_target="tpu_custom_call" | custom-call | flops 1000000000 | tf_op jit(solution)/shard_map/out/pallas_call | solution.py:440
Async XLA Ops:
  0.0 18.1 %collective-permute-start = (f32[4,4096]{1,0:T(4,128)}, f32[4,4096]{1,0:T(4,128)S(1)}, u32[]{:S(2)}, u32[]{:S(2)}) collective-permute-start(f32[4,4096]{1,0:T(4,128)} %own_ref.1), channel_id=1, source_target_pairs={{0,4},{4,8},{8,12},{12,16},{16,20},{20,24},{24,28},{28,32},{32,36}... | collective-permute-start | bytes 196616 | tf_op jit(solution)/shard_map/ppermute | solution.py:369
  0.0 18.1 %collective-permute-start.1 = (f32[4,4096]{1,0:T(4,128)}, f32[4,4096]{1,0:T(4,128)S(1)}, u32[]{:S(2)}, u32[]{:S(2)}) collective-permute-start(f32[4,4096]{1,0:T(4,128)} %own_ref.1), channel_id=1, source_target_pairs={{4,0},{8,4},{12,8},{16,12},{20,16},{24,20},{28,24},{32,28},{36,32}... | collective-permute-start | bytes 196616 | tf_op jit(solution)/shard_map/ppermute | solution.py:370
  5.2 12.9 %copy-start.4 = (f32[4,4096]{1,0:T(4,128)S(1)}, f32[4,4096]{1,0:T(4,128)}, u32[]{:S(2)}) copy-start(f32[4,4096]{1,0:T(4,128)} %own_ref.1) | copy-start | bytes 196612
  5.2 12.9 %copy-start.6 = (s32[64,8]{0,1:T(8,128)S(1)}, s32[64,8]{0,1:T(8,128)}, u32[]{:S(2)}) copy-start(s32[64,8]{0,1:T(8,128)} %param.14) | copy-start | bytes 6148
  8.0 22.0 %copy-start = (f32[2,64,4096]{2,1,0:T(8,128)S(1)}, f32[2,64,4096]{2,1,0:T(8,128)}, u32[]{:S(2)}) copy-start(f32[2,64,4096]{2,1,0:T(8,128)} %blocks_in.1) | copy-start | bytes 6291460
  8.0 26.9 %all-to-all-start = ((f32[64,16,128]{2,1,0:T(8,128)}), f32[64,16,128]{2,1,0:T(8,128)S(1)}, u32[]{:S(2)}, u32[]{:S(2)}) async-start(f32[64,16,128]{2,1,0:T(8,128)} %up.1), calls=%async_computation | async-start | bytes 1048576 | tf_op jit(solution)/shard_map/all_to_all | solution.py:383
  19.4 6.8 %collective-permute-start.2 = (f32[32,8,128]{2,1,0:T(8,128)S(1)}, f32[32,8,128]{2,1,0:T(8,128)S(1)}, u32[]{:S(2)}, u32[]{:S(2)}) collective-permute-start(f32[32,8,128]{2,1,0:T(8,128)S(1)} %get-tuple-element.14), channel_id=1, source_target_pairs={{0,1},{1,2},{2,3},{3,0},{4,5},{5,6},{6,7},{7,4},{8,9},{9,10},{10,1... | collective-permute-start | bytes 393224 | tf_op jit(solution)/shard_map/ppermute | solution.py:401
  20.9 9.1 %collective-permute-start.3 = (f32[32,8,128]{2,1,0:T(8,128)S(1)}, f32[32,8,128]{2,1,0:T(8,128)S(1)}, u32[]{:S(2)}, u32[]{:S(2)}) collective-permute-start(f32[32,8,128]{2,1,0:T(8,128)S(1)} %get-tuple-element.15), channel_id=1, source_target_pairs={{0,2},{1,3},{2,0},{3,1},{4,6},{5,7},{6,4},{7,5},{8,10},{9,11},{10,... | collective-permute-start | bytes 393224 | tf_op jit(solution)/shard_map/ppermute | solution.py:401
  23.7 6.3 %collective-permute-start.4 = (f32[32,8,128]{2,1,0:T(8,128)S(1)}, f32[32,8,128]{2,1,0:T(8,128)S(1)}, u32[]{:S(2)}, u32[]{:S(2)}) collective-permute-start(f32[32,8,128]{2,1,0:T(8,128)S(1)} %get-tuple-element.16), channel_id=1, source_target_pairs={{0,3},{1,0},{2,1},{3,2},{4,7},{5,4},{6,5},{7,6},{8,11},{9,8},{10,9... | collective-permute-start | bytes 393224 | tf_op jit(solution)/shard_map/ppermute | solution.py:401
  30.0 4.9 %copy-start.2 = (f32[8,32,256]{2,1,0:T(8,128)S(1)}, f32[8,32,256]{2,1,0:T(8,128)}, u32[]{:S(2)}) copy-start(f32[8,32,256]{2,1,0:T(8,128)} %refs_3_.1) | copy-start | bytes 786436
  30.0 4.9 %copy-start.3 = (f32[32,2048]{1,0:T(8,128)S(1)}, f32[32,2048]{1,0:T(8,128)}, u32[]{:S(2)}) copy-start(f32[32,2048]{1,0:T(8,128)} %refs_4_.1) | copy-start | bytes 786436
  30.0 4.9 %copy-start.5 = (s32[64,16]{0,1:T(8,128)S(1)}, s32[64,16]{0,1:T(8,128)}, u32[]{:S(2)}) copy-start(s32[64,16]{0,1:T(8,128)} %param.22) | copy-start | bytes 12292
  30.0 4.9 %copy-start.7 = (s32[8,8]{1,0:T(8,128)S(1)}, s32[8,8]{1,0:T(8,128)}, u32[]{:S(2)}) copy-start(s32[8,8]{1,0:T(8,128)} %refs_1_.1) | copy-start | bytes 772
  30.8 7.4 %collective-permute-start.5 = (f32[4,4096]{1,0:T(4,128)S(1)}, f32[4,4096]{1,0:T(4,128)S(1)}, u32[]{:S(2)}, u32[]{:S(2)}) collective-permute-start(f32[4,4096]{1,0:T(4,128)S(1)} %get-tuple-element.18), channel_id=1, source_target_pairs={{0,3},{1,0},{2,1},{3,2},{4,7},{5,4},{6,5},{7,6},{8,11},{9,8},{10,9... | collective-permute-start | bytes 196616 | tf_op jit(solution)/shard_map/ppermute | solution.py:416
  33.1 5.8 %collective-permute-start.6 = (f32[4,4096]{1,0:T(4,128)S(1)}, f32[4,4096]{1,0:T(4,128)S(1)}, u32[]{:S(2)}, u32[]{:S(2)}) collective-permute-start(f32[4,4096]{1,0:T(4,128)S(1)} %get-tuple-element.19), channel_id=1, source_target_pairs={{0,2},{1,3},{2,0},{3,1},{4,6},{5,7},{6,4},{7,5},{8,10},{9,11},{10,... | collective-permute-start | bytes 196616 | tf_op jit(solution)/shard_map/ppermute | solution.py:416
  34.3 5.5 %collective-permute-start.7 = (f32[4,4096]{1,0:T(4,128)S(1)}, f32[4,4096]{1,0:T(4,128)S(1)}, u32[]{:S(2)}, u32[]{:S(2)}) collective-permute-start(f32[4,4096]{1,0:T(4,128)S(1)} %get-tuple-element.20), channel_id=1, source_target_pairs={{0,1},{1,2},{2,3},{3,0},{4,5},{5,6},{6,7},{7,4},{8,9},{9,10},{10,1... | collective-permute-start | bytes 196616 | tf_op jit(solution)/shard_map/ppermute | solution.py:416
  35.0 4.8 %copy-start.1 = (f32[32,4096]{1,0:T(8,128)S(1)}, f32[32,4096]{1,0:T(8,128)}, u32[]{:S(2)}) copy-start(f32[32,4096]{1,0:T(8,128)} %basis_ref.1) | copy-start | bytes 1572868
